TPU v7x, 32 devices: a whole 2x2x4 slice. The times are simulated.
32 devices in a mesh: section: 2 (over x), dp: 4 (over y, core), seq: 4 (over z).
Axes of the slice: x: 2, y: 2, z: 4, core: 2. Of those that a mesh axis runs over, the one named last changes fastest.
Arguments:
- cell_tokens: bfloat16 [8, 2048, 768], P('dp', 'seq'), may hold values from -6 to 6
- cell_lengths: int32 [8, 16], P('dp'), may hold values from 1 to 1537, as said below
- out_grad: bfloat16 [8, 2048, 768], P('dp', 'seq'), may hold values from -6 to 6
- norm1_gain: bfloat16 [2, 768], P('section'), may hold values from 0.25 to 1.75
- norm1_bias: bfloat16 [2, 768], P('section'), may hold values from -1.75 to 1.75
- qkv_weight: bfloat16 [2, 768, 2304], P('section'), may hold values from -0.21875 to 0.21875
- query_bias: bfloat16 [2, 768], P('section'), may hold values from -3 to 3
- value_bias: bfloat16 [2, 768], P('section'), may hold values from -0.625 to 0.625
- out_weight: bfloat16 [2, 768, 768], P('section'), may hold values from -1.25 to 1.25
- out_bias: bfloat16 [2, 768], P('section'), may hold values from -1.75 to 1.75
- norm2_gain: bfloat16 [2, 768], P('section'), may hold values from 0.25 to 1.75
- norm2_bias: bfloat16 [2, 768], P('section'), may hold values from -1.75 to 1.75
- in_weight: bfloat16 [2, 768, 3072], P('section'), may hold values from -0.21875 to 0.21875
- in_bias: bfloat16 [2, 3072], P('section'), may hold values from -3 to 3
- back_weight: bfloat16 [2, 3072, 768], P('section'), may hold values from -0.109375 to 0.109375
- back_bias: bfloat16 [2, 768], P('section'), may hold values from -1.75 to 1.75
Outputs:
- layer_outputs: bfloat16 [2, 8, 2048, 768], P('section', 'dp', 'seq')
- input_grads: float32 [2, 8, 2048, 768], P('section', 'dp', 'seq')
- norm1_gain_grad: float32 [2, 768], P('section', ('dp', 'seq'))
- norm1_bias_grad: float32 [2, 768], P('section', ('dp', 'seq'))
- qkv_weight_grad: float32 [2, 768, 2304], P('section', ('dp', 'seq'))
- query_bias_grad: float32 [2, 768], P('section', ('dp', 'seq'))
- value_bias_grad: float32 [2, 768], P('section', ('dp', 'seq'))
- out_weight_grad: float32 [2, 768, 768], P('section', ('dp', 'seq'))
- out_bias_grad: float32 [2, 768], P('section', ('dp', 'seq'))
- norm2_gain_grad: float32 [2, 768], P('section', ('dp', 'seq'))
- norm2_bias_grad: float32 [2, 768], P('section', ('dp', 'seq'))
- in_weight_grad: float32 [2, 768, 3072], P('section', ('dp', 'seq'))
- in_bias_grad: float32 [2, 3072], P('section', ('dp', 'seq'))
- back_weight_grad: float32 [2, 3072, 768], P('section', ('dp', 'seq'))
- back_bias_grad: float32 [2, 768], P('section', ('dp', 'seq'))
Inputs may be any that keep to these rules, and one draw needn't show every extreme that they name: `cell_lengths`: each row holds 16 cells whose lengths sum to 2048. In each group of 2 consecutive rows, one row drawn from the seed has a cell of 1537 positions that starts within the first 512 positions.
All inputs are finite; a program needn't handle non-finite values.
Results may differ from a plain program's by a relative error of at most 0.014.
Values may be sent and summed in bfloat16 or wider, within the bound.
A program may use at most 384 MiB of HBM per device.

v0:
```python
from functools import partial

import jax
import jax.numpy as jnp
from jax import lax
from jax.experimental import pallas as pl
from jax.experimental.pallas import tpu as pltpu
from jax.sharding import PartitionSpec as P

HEADS = 12


SCALE = 0.125
EPS = 1e-05
MASKED = -1e30


def from_behind(x, axis, by):
    peers = lax.axis_size(axis)
    pairs = [(i, i + by) for i in range(peers) if 0 <= i + by < peers]
    return lax.ppermute(x, axis, pairs)


def norm_rows(values, gain_vec, bias_vec):
    centre = jnp.mean(values, axis=-1, keepdims=True)
    offset = values - centre
    spread = jnp.mean(offset * offset, axis=-1, keepdims=True)
    return offset * lax.rsqrt(spread + EPS) * gain_vec + bias_vec


def row_segments(lengths, row_length):
    limits = jnp.cumsum(lengths, axis=-1)
    places = jnp.arange(row_length, dtype=jnp.int32)
    return jnp.sum((places[None, :, None] >= limits[:, None, :]).astype(jnp.int32), axis=-1)


def split_heads(values):
    return values.reshape(values.shape[0], HEADS, values.shape[1] // HEADS)


def masked_scores(queries, keys_in, seg_query, seg_keys):
    scores = (
        jnp.einsum(
            "qhe,khe->hqk",
            split_heads(queries),
            split_heads(keys_in),
            preferred_element_type=jnp.float32,
        )
        * SCALE
    )
    return jnp.where((seg_query[:, None] == seg_keys[None, :])[None], scores, MASKED)


def softmax_parts(scores):
    highest = jnp.max(scores, axis=-1)
    raised = jnp.exp(scores - highest[..., None])
    summed = jnp.sum(raised, axis=-1)
    return (raised / summed[..., None], highest, summed)


def project_in(inputs, weights):
    normed = norm_rows(inputs, weights[0], weights[1]).astype(jnp.bfloat16)
    joined = jnp.dot(normed, weights[2], preferred_element_type=jnp.float32)
    model_width = inputs.shape[1]
    queries = (joined[:, :model_width] + weights[3]).astype(jnp.bfloat16)
    keys_out = joined[:, model_width : 2 * model_width].astype(jnp.bfloat16)
    values_out = (joined[:, 2 * model_width :] + weights[4]).astype(jnp.bfloat16)
    return (normed, queries, keys_out, values_out)


def attend(queries, keys_all, values_all, seg_own, seg_row):
    soft_probs, highest, summed = softmax_parts(masked_scores(queries, keys_all, seg_own, seg_row))
    low_probs = soft_probs.astype(jnp.bfloat16)
    combined = jnp.einsum(
        "hqk,khe->qhe", low_probs, split_heads(values_all), preferred_element_type=jnp.float32
    )
    return (
        combined.reshape(queries.shape).astype(jnp.bfloat16),
        soft_probs,
        low_probs,
        highest,
        summed,
    )


def finish(inputs, attended, weights):
    resid_sum = (
        inputs + jnp.dot(attended, weights[5], preferred_element_type=jnp.float32) + weights[6]
    )
    normed = norm_rows(resid_sum, weights[7], weights[8]).astype(jnp.bfloat16)
    hidden_pre = jnp.dot(normed, weights[9], preferred_element_type=jnp.float32) + weights[10]
    active = jax.nn.gelu(hidden_pre, approximate=False).astype(jnp.bfloat16)
    result = (
        resid_sum + jnp.dot(active, weights[11], preferred_element_type=jnp.float32) + weights[12]
    )
    return (result, resid_sum, normed, hidden_pre, active)


def store_slot(buffer, item_new, slot_idx, is_valid):
    current = lax.dynamic_index_in_dim(buffer, slot_idx, 0, keepdims=False)
    return lax.dynamic_update_index_in_dim(
        buffer, jnp.where(is_valid, item_new, current), slot_idx, 0
    )


def token_sum(values):
    return jnp.sum(values.astype(jnp.float32), axis=0)


def on_device(
    cell_tokens,
    cell_lengths,
    out_grad,
    norm1_gain,
    norm1_bias,
    qkv_weight,
    query_bias,
    value_bias,
    out_weight,
    out_bias,
    norm2_gain,
    norm2_bias,
    in_weight,
    in_bias,
    back_weight,
    back_bias,
):
    raw_weights = (
        norm1_gain,
        norm1_bias,
        qkv_weight,
        query_bias,
        value_bias,
        out_weight,
        out_bias,
        norm2_gain,
        norm2_bias,
        in_weight,
        in_bias,
        back_weight,
        back_bias,
    )
    weights = tuple(
        (weight[0].astype(jnp.float32) if weight.ndim == 2 else weight[0] for weight in raw_weights)
    )
    sections = lax.axis_size("section")
    section_rank = lax.axis_index("section")
    micro_count, local_len, model_width = cell_tokens.shape
    row_length = local_len * lax.axis_size("seq")
    own_start = lax.axis_index("seq") * local_len
    segments = row_segments(cell_lengths, row_length)
    tick_count = micro_count + sections - 1
    kept_depth = 1

    def row_segs(slot_idx):
        seg_row = lax.dynamic_index_in_dim(segments, slot_idx, 0, keepdims=False)
        return (seg_row, lax.dynamic_slice_in_dim(seg_row, own_start, local_len))

    def forward_tick(tick_now, state_now):
        incoming, kept_in, outputs, kept_keys, kept_values = state_now
        index_now = tick_now - section_rank
        is_valid = (index_now >= 0) & (index_now < micro_count)
        slot_idx = jnp.clip(index_now, 0, micro_count - 1)
        first_in = lax.dynamic_index_in_dim(cell_tokens, slot_idx, 0, keepdims=False)
        layer_in = jnp.where(section_rank == 0, first_in, incoming)
        seg_row, seg_own = row_segs(slot_idx)
        inputs = layer_in.astype(jnp.float32)
        normed, queries, keys_out, values_out = project_in(inputs, weights)
        keys_all, values_all = (
            lax.all_gather(keys_out, "seq", axis=0, tiled=True),
            lax.all_gather(values_out, "seq", axis=0, tiled=True),
        )
        attended = attend(queries, keys_all, values_all, seg_own, seg_row)[0]
        result = finish(inputs, attended, weights)[0].astype(jnp.bfloat16)
        kept_in = store_slot(kept_in, layer_in, slot_idx, is_valid)
        outputs = store_slot(outputs, result, slot_idx, is_valid)
        passed = from_behind(result, "section", 1)
        return (passed, kept_in, outputs, kept_keys, kept_values)

    start_state = (
        jnp.zeros((local_len, model_width), jnp.bfloat16),
        jnp.zeros((micro_count, local_len, model_width), jnp.bfloat16),
        jnp.zeros((micro_count, local_len, model_width), jnp.bfloat16),
        jnp.zeros((kept_depth, row_length, model_width), jnp.bfloat16),
        jnp.zeros((kept_depth, row_length, model_width), jnp.bfloat16),
    )
    ignored, kept_in, outputs, kept_keys, kept_values = lax.fori_loop(
        0, tick_count, forward_tick, start_state
    )

    def backward_tick(tick_now, state_now):
        incoming, in_grads, totals = state_now
        index_now = tick_now - (sections - 1 - section_rank)
        is_valid = (index_now >= 0) & (index_now < micro_count)
        slot_idx = jnp.clip(index_now, 0, micro_count - 1)
        from_out = lax.dynamic_index_in_dim(out_grad, slot_idx, 0, keepdims=False)
        grad_out = jnp.where(section_rank == sections - 1, from_out, incoming).astype(jnp.float32)
        inputs = lax.dynamic_index_in_dim(kept_in, slot_idx, 0, keepdims=False).astype(jnp.float32)
        seg_row, seg_own = row_segs(slot_idx)
        normed_one, queries, keys_out, values_out = project_in(inputs, weights)
        keys_all, values_all = (
            lax.all_gather(keys_out, "seq", axis=0, tiled=True),
            lax.all_gather(values_out, "seq", axis=0, tiled=True),
        )
        attended, soft_probs, low_probs, highest, summed = attend(
            queries, keys_all, values_all, seg_own, seg_row
        )
        result, resid_sum, normed_two, hidden_pre, active = finish(inputs, attended, weights)
        d_result = grad_out.astype(jnp.bfloat16)
        g_back_w = jnp.einsum("tf,td->fd", active, d_result, preferred_element_type=jnp.float32)
        g_back_b = token_sum(d_result)
        d_active = jnp.einsum(
            "td,fd->tf", d_result, weights[11], preferred_element_type=jnp.float32
        )
        gelu_value, gelu_back = jax.vjp(partial(jax.nn.gelu, approximate=False), hidden_pre)
        d_hidden = gelu_back(d_active)[0].astype(jnp.bfloat16)
        g_in_w = jnp.einsum("td,tf->df", normed_two, d_hidden, preferred_element_type=jnp.float32)
        g_in_b = token_sum(d_hidden)
        d_normed_two = jnp.einsum(
            "tf,df->td", d_hidden, weights[9], preferred_element_type=jnp.float32
        )
        norm_value, norm_two_back = jax.vjp(norm_rows, resid_sum, weights[7], weights[8])
        d_resid_norm, g_gain_two, g_bias_two = norm_two_back(d_normed_two)
        d_resid = grad_out + d_resid_norm
        d_proj = d_resid.astype(jnp.bfloat16)
        g_out_w = jnp.einsum("td,te->de", attended, d_proj, preferred_element_type=jnp.float32)
        g_out_b = token_sum(d_proj)
        d_attended = jnp.einsum(
            "te,de->td", d_proj, weights[5], preferred_element_type=jnp.float32
        ).astype(jnp.bfloat16)
        dout_heads = split_heads(d_attended)
        d_probs = jnp.einsum(
            "qhe,khe->hqk", dout_heads, split_heads(values_all), preferred_element_type=jnp.float32
        )
        delta_rows = jnp.sum(soft_probs * d_probs, axis=-1)
        d_scores = (soft_probs * (d_probs - delta_rows[..., None])).astype(jnp.bfloat16)
        d_query = (
            (
                jnp.einsum(
                    "hqk,khe->qhe",
                    d_scores,
                    split_heads(keys_all),
                    preferred_element_type=jnp.float32,
                )
                * SCALE
            )
            .reshape(local_len, model_width)
            .astype(jnp.bfloat16)
        )
        key_part = (
            jnp.einsum(
                "hqk,qhe->khe", d_scores, split_heads(queries), preferred_element_type=jnp.float32
            )
            * SCALE
        ).reshape(row_length, model_width)
        value_part = jnp.einsum(
            "hqk,qhe->khe", low_probs, dout_heads, preferred_element_type=jnp.float32
        ).reshape(row_length, model_width)
        d_keys, d_values = (
            lax.psum_scatter(
                key_part.astype(jnp.bfloat16), "seq", scatter_dimension=0, tiled=True
            ).astype(jnp.float32),
            lax.psum_scatter(
                value_part.astype(jnp.bfloat16), "seq", scatter_dimension=0, tiled=True
            ).astype(jnp.float32),
        )
        d_values_low = d_values.astype(jnp.bfloat16)
        d_joined = jnp.concatenate([d_query, d_keys.astype(jnp.bfloat16), d_values_low], axis=1)
        g_qkv_w = jnp.einsum("td,tf->df", normed_one, d_joined, preferred_element_type=jnp.float32)
        g_q_b = token_sum(d_query)
        g_v_b = token_sum(d_values_low)
        d_normed_one = jnp.einsum(
            "tf,df->td", d_joined, weights[2], preferred_element_type=jnp.float32
        )
        norm_value_one, norm_one_back = jax.vjp(norm_rows, inputs, weights[0], weights[1])
        d_inputs_norm, g_gain_one, g_bias_one = norm_one_back(d_normed_one)
        d_inputs = d_resid + d_inputs_norm
        new_grads = (
            g_gain_one,
            g_bias_one,
            g_qkv_w,
            g_q_b,
            g_v_b,
            g_out_w,
            g_out_b,
            g_gain_two,
            g_bias_two,
            g_in_w,
            g_in_b,
            g_back_w,
            g_back_b,
        )
        totals = tuple(
            (
                running + jnp.where(is_valid, grad_new, 0.0)
                for running, grad_new in zip(totals, new_grads)
            )
        )
        shown = jnp.where(
            section_rank == 0, d_inputs, d_inputs.astype(jnp.bfloat16).astype(jnp.float32)
        )
        in_grads = store_slot(in_grads, shown, slot_idx, is_valid)
        passed = from_behind(d_inputs.astype(jnp.bfloat16), "section", -1)
        return (passed, in_grads, totals)

    back_state = (
        jnp.zeros((local_len, model_width), jnp.bfloat16),
        jnp.zeros((micro_count, local_len, model_width), jnp.float32),
        tuple((jnp.zeros(weight.shape, jnp.float32) for weight in weights)),
    )
    ignored_grad, in_grads, totals = lax.fori_loop(0, tick_count, backward_tick, back_state)
    reduced = lax.psum_scatter(totals, ("dp", "seq"), scatter_dimension=0, tiled=True)
    return (
        outputs[None],
        in_grads[None],
        reduced[0][None],
        reduced[1][None],
        reduced[2][None],
        reduced[3][None],
        reduced[4][None],
        reduced[5][None],
        reduced[6][None],
        reduced[7][None],
        reduced[8][None],
        reduced[9][None],
        reduced[10][None],
        reduced[11][None],
        reduced[12][None],
    )


HEAD = 64
BIG = 1e30
NT = (((1,), (1,)), ((), ()))
F32 = jnp.float32
BF16 = jnp.bfloat16
BLK = 256
CH = 256
FINE = 128
PIECE = 512
UN = 8

def lane_mask(shape, h):
    lane = lax.broadcasted_iota(jnp.int32, shape, len(shape) - 1)
    return (lane < HEAD) if h == 0 else (lane >= HEAD)

def only(x, h):
    return jnp.where(lane_mask(x.shape, h), x, jnp.zeros_like(x))

def fwd_kernel(lo_ref, hi_ref, q_ref, k_ref, v_ref, fq_ref, fk_ref, o_ref, lse_ref):
    i = pl.program_id(0)
    n, w = k_ref.shape
    pairs = w // 128
    lo = lo_ref[i]
    count = hi_ref[i] - lo

    def run(lo, c):
        fq = fq_ref[...]
        at = pl.multiple_of(lo * FINE, FINE)
        pieces = []
        done = 0
        while done < c * FINE:
            size = min(PIECE, c * FINE - done)
            pieces.append(pl.ds(pl.multiple_of(at + done, FINE), size))
            done += size

        def scores(u, rows):
            p, h = divmod(u, 2)
            cols = slice(p * 128, (p + 1) * 128)
            q = q_ref[:, cols] * jnp.asarray(SCALE, BF16)
            qa = jnp.concatenate([only(q, h), fq], axis=1)
            kb = jnp.concatenate([k_ref[rows, cols], fk_ref[rows, :]], axis=1)
            return lax.dot_general(qa, kb, NT, preferred_element_type=F32)

        now = [scores(0, rows) for rows in pieces]
        outs, lses = [], []
        for u in range(2 * pairs):
            p, h = divmod(u, 2)
            cols = slice(p * 128, (p + 1) * 128)
            m = jnp.max(now[0], axis=1, keepdims=True)
            for s in now[1:]:
                m = jnp.maximum(m, jnp.max(s, axis=1, keepdims=True))
            r = None
            later = []
            for s, rows in zip(now, pieces):
                if u + 1 < 2 * pairs:
                    later.append(scores(u + 1, rows))
                pr = jnp.exp(s - m).astype(BF16)
                vb = jnp.concatenate([v_ref[rows, cols], jnp.ones((s.shape[1], 128), BF16)], axis=1)
                part = jnp.dot(pr, vb, preferred_element_type=F32)
                r = part if r is None else r + part
            now = later
            l = r[:, 128:]
            outs.append(r[:, :128] / l)
            lses.append(m + jnp.log(l))
            if h == 1:
                mask = lane_mask((BLK, 128), 0)
                o_ref[:, cols] = jnp.where(mask, outs[0], outs[1]).astype(BF16)
                both = jnp.where(mask, lses[0], lses[1]).T
                lse_ref[p, 0:1, :] = both[0:1, :]
                lse_ref[p, 1:2, :] = both[HEAD:HEAD + 1, :]
                outs, lses = [], []

    most = n // FINE
    below = 0
    for c in sorted({max(BLK // FINE, most * e // 16) for e in (2, 4, 8, 13, 14, 16)}):
        @pl.when((count > below) & (count <= c))
        def _(c=c):
            run(jnp.minimum(lo, most - c), c)
        below = c

def attn_fwd(lo, hi, q, k, v, fq, fk):
    n, w = q.shape
    pairs = w // 128
    blk = lambda i, lo, hi: (i, 0)
    full = lambda i, lo, hi: (0, 0)
    return pl.pallas_call(
        fwd_kernel,
        grid_spec=pltpu.PrefetchScalarGridSpec(
            num_scalar_prefetch=2,
            grid=(n // BLK,),
            in_specs=[pl.BlockSpec((BLK, w), blk), pl.BlockSpec((n, w), full), pl.BlockSpec((n, w), full),
                      pl.BlockSpec((BLK, 128), blk), pl.BlockSpec((n, 128), full)],
            out_specs=[pl.BlockSpec((BLK, w), blk), pl.BlockSpec((pairs, 8, BLK), lambda i, lo, hi: (0, 0, i))],
        ),
        out_shape=[jax.ShapeDtypeStruct((n, w), BF16), jax.ShapeDtypeStruct((pairs, 8, n), F32)],
        compiler_params=pltpu.CompilerParams(vmem_limit_bytes=62 * 2 ** 20),
        name="attn_fwd",
    )(lo, hi, q, k, v, fq, fk)

def bwd_kernel(lo_ref, hi_ref, q_ref, k_ref, v_ref, do_ref, o_ref, lse_ref, fq_ref, fk_ref,
               dq_ref, dk_ref, dv_ref, delta, dqt, dk_acc, dv_acc):
    j = pl.program_id(0)
    nb = pl.num_programs(0)
    n, w = q_ref.shape
    pairs = w // 128

    @pl.when(j == 0)
    def _():
        head = lax.broadcasted_iota(jnp.int32, (16, 128), 0)
        lane = lax.broadcasted_iota(jnp.int32, (16, 128), 1)
        sel = jnp.where(lane // HEAD == head, 1.0, 0.0).astype(BF16)

        def prep(b, c):
            rows = pl.ds(pl.multiple_of(b * CH, CH), CH)
            for p in range(pairs):
                cols = slice(p * 128, (p + 1) * 128)
                prod = do_ref[rows, cols].astype(F32) * o_ref[rows, cols].astype(F32)
                hi = prod.astype(BF16)
                lo = (prod - hi.astype(F32)).astype(BF16)
                d = lax.dot_general(sel, hi, NT, preferred_element_type=F32) + lax.dot_general(sel, lo, NT, preferred_element_type=F32)
                delta[p, :, rows] = d[0:8, :]
                dqt[p, :, rows] = jnp.zeros((128, CH), F32)
            return c
        lax.fori_loop(0, n // CH, prep, 0)

    lo = lo_ref[j]
    count = hi_ref[j] - lo
    dk_acc[...] = jnp.zeros_like(dk_acc)
    dv_acc[...] = jnp.zeros_like(dv_acc)

    def run(first, c):
        rows = pl.ds(pl.multiple_of(first * FINE, FINE), c * FINE)
        units = 2 * pairs

        def scores(u):
            p, h = divmod(u, 2)
            cols = slice(p * 128, (p + 1) * 128)
            kb = jnp.concatenate([only(k_ref[:, cols] * jnp.asarray(SCALE, BF16), h), fk_ref[...]], axis=1)
            qa = jnp.concatenate([q_ref[rows, cols], fq_ref[rows, :]], axis=1)
            s = lax.dot_general(kb, qa, NT, preferred_element_type=F32)
            dp = lax.dot_general(only(v_ref[:, cols], h), do_ref[rows, cols], NT, preferred_element_type=F32)
            return s, dp

        now = scores(0)
        dk, dv = [], []
        for u in range(units):
            p, h = divmod(u, 2)
            cols = slice(p * 128, (p + 1) * 128)
            later = scores(u + 1) if u + 1 < units else None
            s, dp = now
            pr = jnp.exp(s - lse_ref[p, h:h + 1, rows])
            ds = (pr * (dp - delta[p, h:h + 1, rows])).astype(BF16)
            dv.append(jnp.dot(pr.astype(BF16), do_ref[rows, cols], preferred_element_type=F32))
            dk.append(jnp.dot(ds, q_ref[rows, cols], preferred_element_type=F32))
            kt = (k_ref[:, cols] * jnp.asarray(SCALE, BF16)).T
            dqt[p, h * HEAD:(h + 1) * HEAD, rows] += jnp.dot(kt[h * HEAD:(h + 1) * HEAD, :], ds, preferred_element_type=F32)
            now = later
            if h == 1:
                mask = lane_mask((BLK, 128), 0)
                dk_acc[:, cols] += jnp.where(mask, dk[0], dk[1])
                dv_acc[:, cols] += jnp.where(mask, dv[0], dv[1])
                dk, dv = [], []

    @pl.loop(0, count // UN)
    def _(t):
        run(lo + t * UN, UN)

    left = count % UN
    for c in range(1, UN):
        @pl.when(left == c)
        def _(c=c):
            run(lo + (count - left), c)
    dk_ref[...] = (dk_acc[...] * SCALE).astype(BF16)
    dv_ref[...] = dv_acc[...].astype(BF16)

    @pl.when(j == nb - 1)
    def _():
        def fin(b, c):
            rows = pl.ds(pl.multiple_of(b * CH, CH), CH)
            for p in range(pairs):
                dq_ref[rows, p * 128:(p + 1) * 128] = dqt[p, :, rows].T.astype(BF16)
            return c
        lax.fori_loop(0, n // CH, fin, 0)

def attn_bwd(lo, hi, q, k, v, do, o, lse, fq, fk):
    n, w = q.shape
    pairs = w // 128
    full = lambda j, lo, hi: (0, 0)
    blk = lambda j, lo, hi: (j, 0)
    sh = jax.ShapeDtypeStruct((n, w), BF16)
    big = pl.BlockSpec((n, w), full, pipeline_mode=pl.Buffered(1))
    return pl.pallas_call(
        bwd_kernel,
        grid_spec=pltpu.PrefetchScalarGridSpec(
            num_scalar_prefetch=2,
            grid=(n // BLK,),
            in_specs=[big, pl.BlockSpec((BLK, w), blk), pl.BlockSpec((BLK, w), blk), big, big, pl.BlockSpec((pairs, 8, n), lambda j, lo, hi: (0, 0, 0)),
                      pl.BlockSpec((n, 128), full), pl.BlockSpec((BLK, 128), blk)],
            out_specs=[pl.BlockSpec((n, w), full), pl.BlockSpec((BLK, w), blk), pl.BlockSpec((BLK, w), blk)],
            scratch_shapes=[
                pltpu.VMEM((pairs, 8, n), F32),
                pltpu.VMEM((pairs, 128, n), F32),
                pltpu.VMEM((BLK, w), F32),
                pltpu.VMEM((BLK, w), F32),
            ],
        ),
        out_shape=[sh, sh, sh],
        compiler_params=pltpu.CompilerParams(vmem_limit_bytes=62 * 2 ** 20),
        name="attn_bwd",
    )(lo, hi, q, k, v, do, o, lse, fq, fk)

def segment_terms(lengths, n):
    cells = lengths.shape[0]
    place_of = jnp.arange(cells)
    ends = jnp.sum(jnp.where(place_of[:, None] <= place_of[None, :], lengths[:, None], 0), axis=0)
    starts = ends - lengths
    pos = jnp.arange(n, dtype=jnp.int32)[:, None]
    pad = lambda v: jnp.pad(v, (0, 128 - cells))[None, :]
    hot = (pos >= pad(starts)) & (pos < pad(ends))
    used = (jnp.arange(128) < cells)[None, :]
    fq = jnp.where(hot, -BIG, 0.0).astype(BF16)
    fk = jnp.where(used & ~hot, 1.0, 0.0).astype(BF16)
    first = jnp.arange(n // BLK, dtype=jnp.int32)[:, None] * BLK
    lo = jnp.max(jnp.where(starts[None, :] <= first, starts[None, :], 0), axis=1) // FINE
    hi = (jnp.min(jnp.where(ends[None, :] > first + BLK - 1, ends[None, :], n), axis=1) + FINE - 1) // FINE
    return fq, fk, lo.astype(jnp.int32), hi.astype(jnp.int32)


MIB = 2 ** 20
MESH = pl.DeviceIdType.MESH
ANY = pl.BlockSpec(memory_space=pl.ANY)
VMEM = pl.BlockSpec(memory_space=pltpu.VMEM)
DMA = pltpu.SemaphoreType.DMA
TOK = 256
COLS = 768


def sds(shape, dtype):
    return jax.ShapeDtypeStruct(shape, dtype)


def place():
    section, dp, seq = lax.axis_index("section"), lax.axis_index("dp"), lax.axis_index("seq")
    core = lax.rem(dp, 2)
    return section, dp, seq, core


def greet(*devices):
    barrier = pltpu.get_barrier_semaphore()
    for device in devices:
        pl.semaphore_signal(barrier, 1, device_id=device, device_id_type=MESH)
    pl.semaphore_wait(barrier, len(devices))


def column_mates(section, dp, seq, core):
    mates = [(section, dp, lax.rem(seq + t, 4)) for t in range(1, 4)]
    mates += [(section, dp + 1 - 2 * core, lax.rem(seq + t, 4)) for t in range(4)]
    return mates


def remote(src, dst, send_sem, recv_sem, device):
    return pltpu.make_async_remote_copy(
        src_ref=src, dst_ref=dst, send_sem=send_sem, recv_sem=recv_sem,
        device_id=device, device_id_type=MESH,
    )


def span(start, size):
    return pl.ds(pl.multiple_of(start, size), size)


def chunk(i):
    return span(i * TOK, TOK)


def row_norm(values):
    centre = jnp.mean(values, axis=-1, keepdims=True)
    offset = values - centre
    spread = jnp.mean(offset * offset, axis=-1, keepdims=True)
    rstd = lax.rsqrt(spread + EPS)
    return offset * rstd, rstd


def row_norm_back(grad, hat, rstd, gain):
    d_hat = grad * gain
    mean_d = jnp.mean(d_hat, axis=-1, keepdims=True)
    mean_dh = jnp.mean(d_hat * hat, axis=-1, keepdims=True)
    return rstd * (d_hat - mean_d - hat * mean_dh)


def fold(values):
    return jnp.sum(values.reshape(values.shape[0] // 8, 8, values.shape[1]), axis=0)


def up(ref):
    return ref[...].astype(F32)


def gelu_parts(x):
    size = jnp.abs(x)
    d = 1.0 + 0.2316418882 * size
    t = pl.reciprocal(d, approx=True)
    t = t * (2.0 - d * t)
    density = jnp.exp(-0.5 * (x * x)) * 0.3989422804014327
    poly = ((((1.330274429 * t - 1.821255978) * t + 1.781477937) * t - 0.356563782) * t + 0.319381530) * t
    tail = density * poly
    phi = jnp.where(x >= 0.0, 1.0 - tail, tail)
    return x * phi, phi + x * density


def ffn_loads(wo_in, win_in, wback_in, wo, win, wback, sem):
    pairs = [(wo_in, wo)]
    for f in range(win.shape[1] // COLS):
        cols = pl.ds(f * COLS, COLS)
        pairs += [(win_in.at[:, cols], win.at[:, cols]), (wback_in.at[cols], wback.at[cols])]
    return [pltpu.make_async_copy(a, b, sem.at[n]) for n, (a, b) in enumerate(pairs)]


class ToHeads:
    def __init__(self, buf, outs, tokens, width, sems, core, sibling):
        self.buf, self.outs, self.tokens, self.width = buf, outs, tokens, width
        self.own_sem, self.send_sem, self.recv_sem = sems
        self.core, self.sibling = core, sibling

    def _cols(self, part, core):
        return span(part * self.width + core * (self.width // 2), self.width // 2)

    def _sent(self, i, part, owner):
        rows = span(owner * self.tokens + i * TOK, TOK)
        return remote(self.buf.at[chunk(i), self._cols(part, 1 - self.core)], self.outs[part].at[rows],
                      self.send_sem.at[part, i], self.recv_sem.at[part, i], self.sibling)

    def _own(self, i, part):
        rows = span(self.core * self.tokens + i * TOK, TOK)
        return pltpu.make_async_copy(self.buf.at[chunk(i), self._cols(part, self.core)],
                                     self.outs[part].at[rows], self.own_sem.at[part, i])

    def start(self, i):
        for part in range(len(self.outs)):
            self._own(i, part).start()
            self._sent(i, part, self.core).start()

    def wait(self, i):
        for part in range(len(self.outs)):
            self._own(i, part).wait()
            self._sent(i, part, self.core).wait_send()
            self._sent(i, part, 1 - self.core).wait_recv()


class ToTokens:
    def __init__(self, ins, buf, tokens, width, sems, core, sibling):
        self.ins, self.buf, self.tokens, self.width = ins, buf, tokens, width
        self.own_sem, self.send_sem, self.recv_sem = sems
        self.core, self.sibling = core, sibling

    def _cols(self, part, core):
        return span(part * self.width + core * (self.width // 2), self.width // 2)

    def _sent(self, i, part, owner):
        rows = span((1 - self.core) * self.tokens + i * TOK, TOK)
        return remote(self.ins[part].at[rows], self.buf.at[chunk(i), self._cols(part, owner)],
                      self.send_sem.at[part, i], self.recv_sem.at[part, i], self.sibling)

    def _own(self, i, part):
        rows = span(self.core * self.tokens + i * TOK, TOK)
        return pltpu.make_async_copy(self.ins[part].at[rows], self.buf.at[chunk(i), self._cols(part, self.core)],
                                     self.own_sem.at[part, i])

    def start(self, i):
        for part in range(len(self.ins)):
            self._own(i, part).start()
            self._sent(i, part, self.core).start()

    def wait(self, i):
        for part in range(len(self.ins)):
            self._own(i, part).wait()
            self._sent(i, part, 1 - self.core).wait_recv()

    def wait_sent(self, i):
        for part in range(len(self.ins)):
            self._sent(i, part, self.core).wait_send()


def swap_sems(parts, steps):
    return [DMA((parts, steps))] * 3


class Blocks:
    def __init__(self, rows_ref, blocks_ref, gather, sems, section, dp, seq, core):
        self.rows, self.blocks, self.gather = rows_ref, blocks_ref, gather
        self.bounce, self.own_sem, self.send_sem, self.recv_sem = sems
        self.section, self.seq, self.core, self.column = section, seq, core, dp - core
        self.each, self.local, _ = blocks_ref.shape

    def _move(self, j):
        target_core, target_seq = self.seq // self.each, self.core * self.each + j
        slot = lax.rem(self.seq, self.each)
        here = (target_core == self.core) & (target_seq == self.seq)
        if self.gather:
            src, dst = self.blocks.at[j], self.rows.at[span(slot * self.local, self.local)]
        else:
            src, dst = self.rows.at[pl.ds(j * self.local, self.local)], self.blocks.at[slot]
        target = (self.section, self.column + target_core, target_seq)
        return here, src, dst, slot, target

    def start(self, *which):
        for j in which or range(self.each):
            here, src, dst, slot, target = self._move(j)

            @pl.when(here)
            def _():
                pltpu.make_async_copy(src, dst if self.bounce is None else self.bounce, self.own_sem).start()

            @pl.when(jnp.logical_not(here))
            def _():
                remote(src, dst, self.send_sem.at[j], self.recv_sem.at[slot], target).start()

    def wait(self):
        for j in range(self.each):
            here, src, dst, slot, target = self._move(j)

            @pl.when(here)
            def _():
                pltpu.make_async_copy(src, dst if self.bounce is None else self.bounce, self.own_sem).wait()
                if self.bounce is not None:
                    out = pltpu.make_async_copy(self.bounce, dst, self.own_sem)
                    out.start()
                    out.wait()

            @pl.when(jnp.logical_not(here))
            def _():
                remote(src, dst, self.send_sem.at[j], self.recv_sem.at[slot], target).wait_send()
        for j in range(self.each):
            here = (self.seq // self.each == self.core) & (self.core * self.each + j == self.seq)
            mate = (self.section, self.column + 1 - self.core, self.seq)
            if self.gather:
                dst = self.rows.at[pl.ds(j * self.local, self.local)]
                src = self.blocks.at[0]
            else:
                dst = self.blocks.at[j]
                src = self.rows.at[pl.ds(0, self.local)]

            @pl.when(jnp.logical_not(here))
            def _():
                remote(src, dst, self.send_sem.at[0], self.recv_sem.at[j], mate).wait_recv()


def block_scratch(each, local, width):
    return [pltpu.VMEM((local, width), BF16), DMA, DMA((each,)), DMA((each,))]


def project(x, gain, bias, w, qb, vb, buf, rows):
    width = x.shape[1]
    hat, _ = row_norm(x)
    a = (hat * up(gain) + up(bias)).astype(BF16)
    for part in range(3):
        cols = slice(part * width, (part + 1) * width)
        m = jnp.dot(a, w[:, cols], preferred_element_type=F32)
        if part == 0:
            m = m + up(qb)
        if part == 2:
            m = m + up(vb)
        buf[rows, cols] = m.astype(BF16)
    return a


def first_kernel(x_ref, w_in, gain, bias, qb, vb, x_out, q_ref, k_ref, v_ref,
                 xb, w, buf, w_sem, out_sem, own_sem, send_sem, recv_sem, *sems):
    section, dp, seq, core = place()
    sibling = (section, dp + 1 - 2 * core, seq)
    each, local, width = x_ref.shape
    part = local // 2
    column = dp - core
    load = pltpu.make_async_copy(w_in, w, w_sem)
    load.start()
    greet(*[(s, column + c, z) for s in range(2) for c in range(2) for z in range(2 * each)])

    def move(m):
        target_core, target_seq = seq // each, core * each + m
        slot = lax.rem(seq, each)
        here = (section == 0) & (target_core == core) & (target_seq == seq)
        src = x_ref.at[m, span(section * part, part)]
        dst = xb.at[span(slot * local + section * part, part)]
        return here, src, dst, slot, (0, column + target_core, target_seq)

    for m in range(each):
        here, src, dst, slot, target = move(m)

        @pl.when(here)
        def _():
            pltpu.make_async_copy(src, dst, own_sem).start()

        @pl.when(jnp.logical_not(here))
        def _():
            remote(src, dst, send_sem.at[m], recv_sem.at[section, slot], target).start()
    load.wait()

    @pl.when(section == 0)
    def _():
        swap = ToHeads(buf, (q_ref, k_ref, v_ref), each * local, width, sems, core, sibling)

        def out(i):
            return pltpu.make_async_copy(xb.at[chunk(i)], x_out.at[chunk(i)], out_sem.at[i])

        for h in range(2):
            for j in range(each):
                here = (seq // each == core) & (core * each + j == seq) & (h == 0)
                dst = xb.at[pl.ds(j * local + h * part, part)]

                @pl.when(here)
                def _():
                    pltpu.make_async_copy(x_ref.at[0, pl.ds(0, part)], dst, own_sem).wait()

                @pl.when(jnp.logical_not(here))
                def _():
                    remote(x_ref.at[0, pl.ds(0, part)], dst, send_sem.at[0], recv_sem.at[h, j], sibling).wait_recv()

                for i in range((j * local + h * part) // TOK, (j * local + (h + 1) * part) // TOK):
                    rows = slice(i * TOK, (i + 1) * TOK)
                    project(xb[rows, :].astype(F32), gain, bias, w, qb, vb, buf, rows)
                    out(i).start()
                    swap.start(i)
        for i in range(each * local // TOK):
            out(i).wait()
            swap.wait(i)

    for m in range(each):
        here, src, dst, slot, target = move(m)

        @pl.when(jnp.logical_not(here))
        def _():
            remote(src, dst, send_sem.at[m], recv_sem.at[section, slot], target).wait_send()


def first_call(x, w, gain, bias, qb, vb):
    each, local, width = x.shape
    tokens = each * local
    steps = tokens // TOK
    out = sds((2 * tokens, width // 2), BF16)
    return pl.pallas_call(
        first_kernel,
        in_specs=[ANY, ANY] + [VMEM] * 4,
        out_specs=[ANY] * 4,
        out_shape=[sds((tokens, width), BF16), out, out, out],
        scratch_shapes=[
            pltpu.VMEM((tokens, width), BF16), pltpu.VMEM(w.shape, BF16), pltpu.VMEM((tokens, 3 * width), BF16),
            DMA, DMA((steps,)), DMA, DMA((each,)), DMA((2, each))] + swap_sems(3, steps),
        compiler_params=pltpu.CompilerParams(collective_id=1, has_side_effects=True, vmem_limit_bytes=62 * MIB),
        name="rows_qkv",
    )(x, w, gain, bias, qb, vb)


def feed(i, out, att, x, wo, win, wback, bo, g2, b2, bi, bb, keep=None, ready=None):
    rows = chunk(i)
    hidden = win.shape[1]
    if ready:
        ready[0].wait()
    resid = x[rows, :].astype(F32) + up(bo) + jnp.dot(att[rows, :], wo[...], preferred_element_type=F32)
    hat, rstd = row_norm(resid)
    c = (hat * up(g2) + up(b2)).astype(BF16)
    if keep is not None:
        resid_b, slope_b, att_t, c_t, act_t = keep
        resid_b[rows, :] = resid
        att_t[:, rows] = att[rows, :].T
        c_t[:, rows] = c.T
    total = resid + up(bb)
    yield
    for f in range(hidden // COLS):
        cols = slice(f * COLS, (f + 1) * COLS)
        if ready:
            ready[1 + 2 * f].wait()
            ready[2 + 2 * f].wait()
        inner = jnp.dot(c, win[:, cols], preferred_element_type=F32) + bi[:, cols].astype(F32)
        yield
        active, slope = gelu_parts(inner)
        active = active.astype(BF16)
        if keep is not None:
            slope_b[rows, cols] = slope.astype(BF16)
            act_t[cols, rows] = active.T
        total = total + jnp.dot(active, wback[cols, :], preferred_element_type=F32)
        yield
    out[rows, :] = total.astype(BF16)


def feed_back(i, dy, slope_b, resid_b, wo, win, wback, g2, di_b, dr_b, dp_b, da_b, sums):
    rows = chunk(i)
    hidden = win.shape[1]
    g = dy.astype(F32)
    d_c = jnp.zeros(dy.shape, F32)
    yield
    for f in range(hidden // COLS):
        cols = slice(f * COLS, (f + 1) * COLS)
        d_active = lax.dot_general(dy, wback[cols, :], NT, preferred_element_type=F32)
        yield
        d_inner = d_active * slope_b[rows, cols].astype(F32)
        if sums:
            sums[3][:, cols] += fold(d_inner)
        d_inner = d_inner.astype(BF16)
        if di_b is not None:
            di_b[rows, cols] = d_inner
        d_c = d_c + lax.dot_general(d_inner, win[:, cols], NT, preferred_element_type=F32)
        yield
    hat, rstd = row_norm(resid_b[rows, :])
    d_resid = g + row_norm_back(d_c, hat, rstd, up(g2))
    d_proj = d_resid.astype(BF16)
    dr_b[rows, :] = d_resid
    if sums:
        s_gain, s_bias, s_out, _, s_back = sums
        s_gain[...] += fold(d_c * hat)
        s_bias[...] += fold(d_c)
        s_out[...] += fold(d_resid)
        s_back[...] += fold(g)
    if dp_b is not None:
        dp_b[rows, :] = d_proj
    da_b[rows, :] = lax.dot_general(d_proj, wo[...], NT, preferred_element_type=F32).astype(BF16)


def in_turns(*parts):
    parts = list(parts)
    while parts:
        for part in list(parts):
            if next(part, part) is part:
                parts.remove(part)


def pass_kernel(o_ref, x_ref, g_ref, wo_in, win_in, wback_in, wqkv_in, bo, g2, b2, bi, bb, g1, b1, qb, vb,
                x_out, g_out, n_out, q_ref, k_ref, v_ref,
                wo, win, wback, wqkv, att, yb, xn, buf, w_sem, x_send, x_recv, x_sem, *sems):
    section, dp, seq, core = place()
    sibling = (section, dp + 1 - 2 * core, seq)
    across = (1 - section, dp, seq)
    tokens, width = x_ref.shape
    steps = tokens // TOK
    loads = ffn_loads(wo_in, win_in, wback_in, wo, win, wback, w_sem)
    load_qkv = pltpu.make_async_copy(wqkv_in, wqkv, w_sem.at[len(loads)])
    loads[0].start()
    greet(across, *column_mates(section, dp, seq, core))
    to_tokens = ToTokens((o_ref,), att, tokens, width, sems[:3], core, sibling)
    to_heads = ToHeads(buf, (q_ref, k_ref, v_ref), tokens, width, sems[3:6], core, sibling)
    blocks = Blocks(g_out, g_ref, True, sems[6:10], section, dp, seq, core)
    to_tokens.start(0)
    for load in loads[1:]:
        load.start()

    @pl.loop(1, steps)
    def _(i):
        to_tokens.start(i)

    load_qkv.start()

    @pl.when(section == 1)
    def _():
        blocks.start()

    def passed(i):
        return remote(yb.at[chunk(i)], xn.at[chunk(i)], x_send.at[i], x_recv.at[i], across)

    def kept(i):
        return pltpu.make_async_copy(xn.at[chunk(i)], x_out.at[chunk(i)], x_sem.at[i])

    def send_chunk(i, ready=None):
        in_turns(feed(i, yb, att, x_ref, wo, win, wback, bo, g2, b2, bi, bb, ready=ready))
        passed(i).start()
        xn[chunk(i), :] = x_ref[chunk(i), :]

    to_tokens.wait(0)

    @pl.when(section == 0)
    def _():
        send_chunk(0, loads)

    @pl.when(section == 1)
    def _():
        for load in loads:
            load.wait()

    @pl.loop(1, steps)
    def _(i):
        to_tokens.wait(i)

        @pl.when(section == 0)
        def _():
            send_chunk(i)

    load_qkv.wait()

    @pl.loop(0, steps)
    def _(i):
        @pl.when(section == 1)
        def _():
            passed(i).wait_recv()

        kept(i).start()
        a = project(xn[chunk(i), :].astype(F32), g1, b1, wqkv, qb, vb, buf, chunk(i))
        n_out[:, chunk(i)] = a.T
        to_heads.start(i)

    @pl.loop(0, steps)
    def _(i):
        to_tokens.wait_sent(i)
        to_heads.wait(i)
        kept(i).wait()

        @pl.when(section == 0)
        def _():
            passed(i).wait_send()

    @pl.when(section == 1)
    def _():
        blocks.wait()


def pass_call(o, x, g, wo, win, wback, wqkv, vectors):
    tokens, width = x.shape
    steps = tokens // TOK
    each = g.shape[0]
    out = sds((2 * tokens, width // 2), BF16)
    low = sds(x.shape, BF16)
    low_buf = pltpu.VMEM(x.shape, BF16)
    return pl.pallas_call(
        pass_kernel,
        in_specs=[ANY, VMEM, ANY, ANY, ANY, ANY, ANY] + [VMEM] * len(vectors),
        out_specs=[ANY, ANY, VMEM, ANY, ANY, ANY],
        out_shape=[low, low, sds((width, tokens), BF16), out, out, out],
        scratch_shapes=[pltpu.VMEM(w.shape, BF16) for w in (wo, win, wback, wqkv)]
        + [low_buf, low_buf, low_buf, pltpu.VMEM((tokens, 3 * width), BF16),
           DMA((2 + 2 * (win.shape[1] // COLS),)), DMA((steps,)), DMA((steps,)), DMA((steps,))]
        + swap_sems(1, steps) + swap_sems(3, steps) + block_scratch(each, tokens // each, width),
        compiler_params=pltpu.CompilerParams(collective_id=2, has_side_effects=True, vmem_limit_bytes=62 * MIB),
        name="ffn_pass_qkv",
    )(o, x, g, wo, win, wback, wqkv, *vectors)


def turn_kernel(o_ref, x_ref, g_ref, wo_in, win_in, wback_in, bo, g2, b2, bi, bb,
                y_out, resid_out, slope_out, att_out, c_out, act_out, dr_out, da_ref,
                wo, win, wback, att, yb, resid_b, slope_b, att_t, c_t, act_t, dr_b, da_b,
                w_sem, out_sem, *sems):
    section, dp, seq, core = place()
    sibling = (section, dp + 1 - 2 * core, seq)
    tokens, width = x_ref.shape
    steps = tokens // TOK
    loads = ffn_loads(wo_in, win_in, wback_in, wo, win, wback, w_sem)
    loads[0].start()
    greet(sibling)
    to_tokens = ToTokens((o_ref,), att, tokens, width, sems[:3], core, sibling)
    to_heads = ToHeads(da_b, (da_ref,), tokens, width, sems[3:6], core, sibling)
    to_tokens.start(0)
    for load in loads[1:]:
        load.start()

    @pl.loop(1, steps)
    def _(i):
        to_tokens.start(i)

    def copies(i, which, at, turned=False):
        where = (slice(None), chunk(i)) if turned else (chunk(i),)
        return [pltpu.make_async_copy(b.at[where], o.at[where], out_sem.at[at + n, i]) for n, (b, o) in enumerate(which)]

    def results(i):
        return copies(i, ((yb, y_out), (resid_b, resid_out), (slope_b, slope_out)), 0) + copies(
            i, ((att_t, att_out), (c_t, c_out), (act_t, act_out)), 3, True)

    def back_results(i):
        return copies(i, ((dr_b, dr_out),), 6)

    def forward(i, ready=None):
        return feed(i, yb, att, x_ref, wo, win, wback, bo, g2, b2, bi, bb, (resid_b, slope_b, att_t, c_t, act_t), ready)

    def backward(i):
        return feed_back(i, g_ref[chunk(i), :], slope_b, resid_b, wo, win, wback, g2, None, dr_b, None, da_b, None)

    to_tokens.wait(0)
    in_turns(forward(0, loads))
    for copy in results(0):
        copy.start()

    @pl.loop(1, steps)
    def _(i):
        to_tokens.wait(i)
        in_turns(forward(i))
        in_turns(backward(i - 1))
        to_heads.start(i - 1)
        for copy in results(i) + back_results(i - 1):
            copy.start()

    in_turns(backward(steps - 1))
    to_heads.start(steps - 1)
    for copy in back_results(steps - 1):
        copy.start()

    @pl.loop(0, steps)
    def _(i):
        to_tokens.wait_sent(i)
        to_heads.wait(i)
        for copy in results(i) + back_results(i):
            copy.wait()


def turn_call(o, x, g, wo, win, wback, vectors):
    tokens, width = x.shape
    hidden = win.shape[1]
    steps = tokens // TOK
    low, full = sds(x.shape, BF16), sds(x.shape, F32)
    turned = sds((width, tokens), BF16)
    outs = [low, full, sds((tokens, hidden), BF16), turned, turned, sds((hidden, tokens), BF16), full]
    buf = lambda s: pltpu.VMEM(s.shape, s.dtype)
    return pl.pallas_call(
        turn_kernel,
        in_specs=[ANY, VMEM, VMEM, ANY, ANY, ANY] + [VMEM] * len(vectors),
        out_specs=[ANY] * 8,
        out_shape=outs + [sds((2 * tokens, width // 2), BF16)],
        scratch_shapes=[buf(wo), buf(win), buf(wback), buf(low)] + [buf(s) for s in outs] + [buf(low)]
        + [DMA((1 + 2 * (hidden // COLS),)), DMA((7, steps))] + swap_sems(1, steps) + swap_sems(1, steps),
        compiler_params=pltpu.CompilerParams(collective_id=3, has_side_effects=True, vmem_limit_bytes=62 * MIB),
        name="ffn_turn",
    )(o, x, g, wo, win, wback, *vectors)


def input_back(i, dj, dr, x, w, gain, sums):
    rows = chunk(i)
    width = x.shape[1]
    d_a = lax.dot_general(dj[rows, :], w[...], NT, preferred_element_type=F32)
    hat, rstd = row_norm(x[rows, :].astype(F32))
    if sums:
        s_gain, s_bias, s_q, s_v = sums
        s_q[...] += fold(dj[rows, :width].astype(F32))
        s_v[...] += fold(dj[rows, 2 * width:].astype(F32))
        s_gain[...] += fold(d_a * hat)
        s_bias[...] += fold(d_a)
    return (dr[rows, :] + row_norm_back(d_a, hat, rstd, up(gain))).astype(BF16)


def back_kernel(dq_ref, dk_ref, dv_ref, dr_ref, x_ref, y_ref, g_in, slope_in, resid_in, c_in, act_in,
                wqkv_in, wo_in, win_in, wback_in, g1, g2,
                y_out, dr_out, dp_out, da_ref, *rest):
    rest = list(rest)
    shares = [rest.pop(0) for _ in range(4)]
    y_shares = [rest.pop(0) for _ in range(2)]
    s_gain, s_bias, s_out, s_in, s_back = [rest.pop(0) for _ in range(5)]
    wqkv, wo, win, wback, dj, dx, gb, di, dr, dp, da_b, c_t, act_t, grad_in, grad_back = [rest.pop(0) for _ in range(15)]
    (w_sem, in_sem, a_sem, t_sem, out_sem, g_sem, x_send, x_recv, ready, r_send, r_recv, r_out) = rest[:12]
    sems = rest[12:]
    section, dp_index, seq, core = place()
    sibling = (section, dp_index + 1 - 2 * core, seq)
    across = (1 - section, dp_index, seq)
    tokens, width = gb.shape
    hidden = win.shape[1]
    steps = tokens // TOK
    blocks_of = hidden // COLS
    x_b, dr_in = da_b, grad_back
    loads = [pltpu.make_async_copy(a, b, w_sem.at[n]) for n, (a, b) in enumerate(
        ((wqkv_in, wqkv), (wback_in, wback), (win_in, win), (wo_in, wo), (c_in, c_t)))]

    def kept(i):
        return [pltpu.make_async_copy(a.at[chunk(i)], b.at[chunk(i)], in_sem.at[n, i])
                for n, (a, b) in enumerate(((slope_in, di), (resid_in, dr)))]

    def turned(i):
        return pltpu.make_async_copy(act_in.at[:, chunk(i)], act_t.at[lax.rem(i, 2)], t_sem.at[i])

    def given(i):
        return [pltpu.make_async_copy(a.at[chunk(i)], b.at[chunk(i)], a_sem.at[n, i])
                for n, (a, b) in enumerate(((x_ref, x_b), (dr_ref, dr_in)))]

    def last(i):
        return pltpu.make_async_copy(g_in.at[chunk(i)], gb.at[chunk(i)], g_sem.at[i])

    def passed(i):
        return remote(dx.at[chunk(i)], gb.at[chunk(i)], x_send.at[i], x_recv.at[i], across)

    def results(i):
        return [pltpu.make_async_copy(b.at[chunk(i)], o.at[chunk(i)], out_sem.at[n, i])
                for n, (b, o) in enumerate(((dr, dr_out), (dp, dp_out)))]

    @pl.when(section == 1)
    def _():
        loads[0].start()

    greet(across, *column_mates(section, dp_index, seq, core))
    to_tokens = ToTokens((dq_ref, dk_ref, dv_ref), dj, tokens, width, sems[:3], core, sibling)
    to_heads = ToHeads(da_b, (da_ref,), tokens, width, sems[3:6], core, sibling)
    blocks = Blocks(y_ref, y_out, False, sems[6:10], section, dp_index, seq, core)

    @pl.when(section == 1)
    def _():
        @pl.loop(0, steps)
        def _(i):
            to_tokens.start(i)
            for copy in given(i):
                copy.start()

        loads[0].wait()

        @pl.loop(0, steps)
        def _(i):
            to_tokens.wait(i)
            for copy in given(i):
                copy.wait()
            last(i).start()
            dx[chunk(i), :] = input_back(i, dj, dr_in, x_b, wqkv, g1, None)
            passed(i).start()

    for load in loads[1:]:
        load.start()

    @pl.loop(0, steps)
    def _(i):
        for copy in kept(i):
            copy.start()

    for i in range(2):
        turned(i).start()
    blocks.start()
    sums = (s_gain, s_bias, s_out, s_in, s_back)
    for s in sums + (grad_in, grad_back):
        s[...] = jnp.zeros_like(s)
    for load in loads[1:]:
        load.wait()

    def grad_block(i, n):
        part = span(n % blocks_of * COLS, COLS) if not isinstance(n, int) else pl.ds(n % blocks_of * COLS, COLS)
        if n < blocks_of:
            grad_in[:, part] += jnp.dot(c_t[:, chunk(i)], di[chunk(i), part], preferred_element_type=F32)
        else:
            grad_back[part, :] += jnp.dot(act_t[lax.rem(i, 2), part, :], gb[chunk(i), :], preferred_element_type=F32)

    def feed_step(i):
        for copy in kept(i):
            copy.wait()

        @pl.when(section == 0)
        def _():
            passed(i).wait_recv()

        @pl.when(section == 1)
        def _():
            last(i).wait()

        in_turns(feed_back(i, gb[chunk(i), :], di, dr, wo, win, wback, g2, di, dr, dp, da_b, sums))
        to_heads.start(i)
        for copy in results(i):
            copy.start()

    @pl.loop(0, steps - 1)
    def _(i):
        feed_step(i)
        turned(i).wait()
        for n in range(2 * blocks_of):
            grad_block(i, n)

        @pl.when(i + 2 < steps)
        def _():
            turned(i + 2).start()

    end = steps - 1
    feed_step(end)
    pl.semaphore_signal(ready, 1, device_id=sibling, device_id_type=MESH)
    turned(end).wait()
    pl.semaphore_wait(ready, 1)

    size_in, size_back = width // 16, hidden // 16

    def sent_in(n, yy):
        cols = pl.ds(n * COLS, COLS)
        return remote(win.at[pl.ds(yy * 4 * size_in, 4 * size_in), cols],
                      win.at[pl.ds((2 + yy) * 4 * size_in, 4 * size_in), cols],
                      r_send.at[2 * n + yy], r_recv.at[2 * n + yy], sibling)

    def sent_back(n):
        yy = n // 2
        return remote(wback.at[pl.ds(yy * COLS, COLS)], wback.at[pl.ds((2 + yy) * COLS, COLS)],
                      r_send.at[2 * blocks_of + yy], r_recv.at[2 * blocks_of + yy], sibling)

    def write_in(t, yy):
        rows = span((2 + yy) * 4 * size_in + lax.rem(seq + t, 4) * size_in, size_in)
        return pltpu.make_async_copy(win.at[rows], shares[t].at[pl.ds(yy * size_in, size_in)], r_out.at[t, yy])

    def write_back(t):
        yy = (dp_index // 2 + t) % 2
        return pltpu.make_async_copy(wback.at[span((2 + yy) * COLS, COLS)], y_shares[t], r_out.at[4, t])

    for n in range(blocks_of):
        grad_block(end, n)
        cols = slice(n * COLS, (n + 1) * COLS)
        for yy in range(2):
            win[yy * 4 * size_in:(yy + 1) * 4 * size_in, cols] = grad_in[core_rows(size_in, yy, 1 - core), cols].astype(BF16)
            sent_in(n, yy).start()
    for n in range(blocks_of):
        grad_block(end, blocks_of + n)
        if n % 2 == 1:
            yy = n // 2
            wback[yy * COLS:(yy + 1) * COLS, :] = grad_back[core_rows(size_back, yy, 1 - core), :].astype(BF16)
            sent_back(n).start()
    for n in range(blocks_of):
        cols = slice(n * COLS, (n + 1) * COLS)
        for yy in range(2):
            sent_in(n, yy).wait_recv()
            rows = slice((2 + yy) * 4 * size_in, (3 + yy) * 4 * size_in)
            win[rows, cols] = (grad_in[core_rows(size_in, yy, core), cols] + win[rows, cols].astype(F32)).astype(BF16)
    for yy in range(2):
        for t in range(4):
            write_in(t, yy).start()
    for yy in range(2):
        sent_back(2 * yy).wait_recv()
        rows = slice((2 + yy) * COLS, (3 + yy) * COLS)
        wback[rows, :] = (grad_back[core_rows(size_back, yy, core), :] + wback[rows, :].astype(F32)).astype(BF16)
    for t in range(2):
        write_back(t).start()

    @pl.loop(0, steps)
    def _(i):
        to_heads.wait(i)
        for copy in results(i):
            copy.wait()

        @pl.when(section == 1)
        def _():
            to_tokens.wait_sent(i)
            passed(i).wait_send()

    for yy in range(2):
        for n in range(blocks_of):
            sent_in(n, yy).wait_send()
        sent_back(2 * yy).wait_send()
        write_back(yy).wait()
        for t in range(4):
            write_in(t, yy).wait()
    blocks.wait()


def back_call(dq, dk, dv, dr, x, y, g, slope, resid, c_t, act_t, wqkv, wo, win, wback, g1, g2, each):
    tokens, width = x.shape
    hidden = win.shape[1]
    steps = tokens // TOK
    blocks_of = hidden // COLS
    low, full, wide = sds(x.shape, BF16), sds(x.shape, F32), sds((tokens, hidden), BF16)
    one = sds((8, width), F32)
    buf = lambda s: pltpu.VMEM(s.shape, s.dtype)
    shares = [sds((width // 8, hidden), BF16)] * 4 + [sds((hidden // 4, width), BF16)] * 2
    return pl.pallas_call(
        back_kernel,
        in_specs=[ANY] * 15 + [VMEM, VMEM],
        out_specs=[ANY] * 10 + [VMEM] * 5,
        out_shape=[sds((each, tokens // each, width), BF16), full, low, sds((2 * tokens, width // 2), BF16)]
        + shares + [one, one, one, sds((8, hidden), F32), one],
        scratch_shapes=[buf(wqkv), buf(wo), buf(win), buf(wback), pltpu.VMEM((tokens, 3 * width), BF16),
                        buf(low), buf(low), buf(wide), buf(full), buf(low), buf(low), buf(c_t),
                        pltpu.VMEM((2, hidden, TOK), BF16), pltpu.VMEM((width, hidden), F32), pltpu.VMEM((hidden, width), F32),
                        DMA((5,)), DMA((2, steps)), DMA((2, steps)), DMA((steps,)), DMA((2, steps)), DMA((steps,)),
                        DMA((steps,)), DMA((steps,)), pltpu.SemaphoreType.REGULAR,
                        DMA((2 * blocks_of + 2,)), DMA((2 * blocks_of + 2,)), DMA((5, 2))]
        + swap_sems(3, steps) + swap_sems(1, steps) + block_scratch(each, tokens // each, width),
        compiler_params=pltpu.CompilerParams(collective_id=4, has_side_effects=True, vmem_limit_bytes=62 * MIB),
        name="qkv_back_pass",
    )(dq, dk, dv, dr, x, y, g, slope, resid, c_t, act_t, wqkv, wo, win, wback, g1, g2)


def core_rows(size, yy, core):
    return span((2 * yy + core) * 4 * size, 4 * size)


def attn_plan(width):
    return [(width, width, 0, 0)] + [(width, width, 1, i * width) for i in range(3)]


def piece(left, right, at, cols, out):
    step = min(left.shape[0], 1024)

    @pl.loop(0, left.shape[0] // step)
    def _(r):
        block = span(r * step, step)
        out[block, :] = jnp.dot(left[block, :], right[:, at:at + cols], preferred_element_type=F32).astype(BF16)


def grads_kernel(n_small, *refs):
    refs = list(refs)
    d_parts = [refs.pop(0) for _ in range(3)]
    dr_ref, x_ref, w_in, g1 = [refs.pop(0) for _ in range(4)]
    lefts = [refs.pop(0) for _ in range(2)]
    rights = [refs.pop(0)]
    ffn_in = [refs.pop(0) for _ in range(4)]
    back_in = [refs.pop(0) for _ in range(2)]
    sums = [refs.pop(0) for _ in range(n_small)]
    outs = [refs.pop(0) for _ in range(2)]
    ffn_out, back_out = refs.pop(0), refs.pop(0)
    small_out, dx_out = refs.pop(0), refs.pop(0)
    left_buf = [refs.pop(0) for _ in range(2)]
    right_buf = [refs.pop(0) for _ in range(2)]
    w, dr, x, dxb = [refs.pop(0) for _ in range(4)]
    own_sums = [refs.pop(0) for _ in range(4)]
    dj = right_buf[1]
    ffn_buf, ffn_rec, back_buf, back_rec = [refs.pop(0) for _ in range(4)]
    width, tokens = lefts[0].shape
    plan = attn_plan(width)
    buf1 = [refs.pop(0) for _ in plan]
    rec1 = [refs.pop(0) for _ in plan]
    rec2 = [refs.pop(0) for _ in plan]
    rec3 = [refs.pop(0) for _ in plan]
    small, small1, small2, small3 = [refs.pop(0) for _ in range(4)]
    (load_sem, s1_send, s1_recv, s2_send, s2_recv, s3_send, s3_recv,
     m_send, m_recv, f_send, f_recv, f_load, b_load, b_send, b_recv, in_sem) = refs[:16]

    section, dp, seq, core = place()
    y = dp // 2
    sibling = (section, dp + 1 - 2 * core, seq)
    across_y = (section, dp + 2 - 4 * y, seq)
    along = [(section, dp, lax.rem(seq + t, 4)) for t in range(1, 4)]
    count = len(plan)
    steps = tokens // TOK
    load_w = pltpu.make_async_copy(w_in, w, load_sem.at[1, 1])
    loads = [[pltpu.make_async_copy(lefts[0], left_buf[0], load_sem.at[0, 0]),
              pltpu.make_async_copy(rights[0], right_buf[0], load_sem.at[1, 0])],
             [pltpu.make_async_copy(lefts[1], left_buf[1], load_sem.at[0, 1])]]

    def given(i):
        return [pltpu.make_async_copy(a.at[chunk(i)], b.at[chunk(i)], in_sem.at[n, i])
                for n, (a, b) in enumerate(((x_ref, x), (dr_ref, dr)))]

    greet(across_y, *column_mates(section, dp, seq, core))
    to_tokens = ToTokens(d_parts, dj, tokens, width, refs[16:19], core, sibling)
    blocks = Blocks(dxb, dx_out, False, [None] + refs[19:22], section, dp, seq, core)
    ffn_loads = [pltpu.make_async_copy(ffn_in[t], ffn_buf.at[t], f_load.at[t]) for t in range(4)]
    back_loads = [pltpu.make_async_copy(back_in[t], back_buf.at[t], b_load.at[t]) for t in range(2)]
    for load in back_loads:
        load.start()

    @pl.loop(0, steps)
    def _(i):
        to_tokens.start(i)
        for copy in given(i):
            copy.start()

    load_w.start()
    for pair in loads:
        for load in pair:
            load.start()
    for load in ffn_loads:
        load.start()

    def ffn_half(yy):
        rows = ffn_rec.shape[0]
        return span(yy * rows, rows)

    def ffn_sent():
        return remote(ffn_buf.at[0, ffn_half(1 - y)], ffn_rec, f_send, f_recv, across_y)

    def ffn_sum(yy):
        rows = ffn_half(yy)
        total = ffn_buf[0, rows, :].astype(F32)
        for t in range(1, 4):
            total = total + ffn_buf[t, rows, :].astype(F32)
        return total

    next_z = seq + 1 - 2 * lax.rem(seq, 2)
    far_z = lax.rem(seq + 2, 4)

    def back_rows(zz):
        rows = back_rec.shape[1]
        return span(zz * rows, rows)

    def back_near(t):
        return remote(back_buf.at[0, back_rows(lax.rem(next_z + 2 * t, 4))], back_rec.at[t],
                      b_send.at[t], b_recv.at[t], (section, dp, next_z))

    def back_far():
        return remote(back_buf.at[0, back_rows(far_z)], back_rec.at[2], b_send.at[2], b_recv.at[2], (section, dp, far_z))

    def back_add(rows, other):
        back_buf[0, rows, :] = (back_buf[0, rows, :].astype(F32) + other.astype(F32)).astype(BF16)

    size = width // 16

    def half(yy):
        return span(yy * 4 * size, 4 * size)

    def first(p, yy):
        return remote(buf1[p].at[core_rows(size, yy, 1 - core)], rec1[p].at[half(yy)],
                      s1_send.at[p, yy], s1_recv.at[p, yy], sibling)

    def second(p):
        return remote(rec1[p].at[half(1 - y)], rec2[p], s2_send.at[p], s2_recv.at[p], across_y)

    def shard(zz):
        return span(y * 4 * size + zz * size, size)

    def third(p, t):
        target = (section, dp, next_z)
        return remote(rec1[p].at[shard(lax.rem(next_z + 2 * t, 4))], rec3[p].at[t],
                      s3_send.at[p, t], s3_recv.at[p, t], target)

    def fourth(p):
        return remote(rec1[p].at[shard(far_z)], rec3[p].at[2], s3_send.at[p, 2], s3_recv.at[p, 2], (section, dp, far_z))

    def reduce_core(p):
        for yy in range(2):
            first(p, yy).wait_recv()
            total = buf1[p][core_rows(size, yy, core), :].astype(F32) + rec1[p][half(yy), :].astype(F32)
            rec1[p][half(yy), :] = total.astype(BF16)
        second(p).start()

    def reduce_y(p):
        second(p).wait_recv()
        mine = half(y)
        rec1[p][mine, :] = (rec1[p][mine, :].astype(F32) + rec2[p][...].astype(F32)).astype(BF16)
        for t in range(2):
            third(p, t).start()

    def reduce_next(p):
        for t, zz in enumerate((seq, far_z)):
            third(p, t).wait_recv()
            rec1[p][shard(zz), :] = (rec1[p][shard(zz), :].astype(F32) + rec3[p][t].astype(F32)).astype(BF16)
        fourth(p).start()

    def reduce_far(p):
        rows, cols, t_out, at = plan[p]
        fourth(p).wait_recv()
        outs[t_out][:, at:at + cols] = rec1[p][shard(seq), :].astype(F32) + rec3[p][2].astype(F32)

    for load in back_loads:
        load.wait()
    back_buf[0] = (back_buf[0].astype(F32) + back_buf[1].astype(F32)).astype(BF16)
    for t in range(2):
        back_near(t).start()

    for s in own_sums:
        s[...] = jnp.zeros_like(s)
    load_w.wait()
    per = steps // dx_out.shape[0]
    for j in range(dx_out.shape[0]):
        @pl.loop(j * per, (j + 1) * per)
        def _(i):
            to_tokens.wait(i)
            for copy in given(i):
                copy.wait()
            dxb[chunk(i), :] = input_back(i, dj, dr, x, w, g1, own_sums)

        blocks.start(j)

    line = 0
    for s in own_sums + sums:
        row = jnp.sum(s[...], axis=0, keepdims=True)
        for t in range(s.shape[1] // 128):
            small[line:line + 1, :] = row[:, t * 128:(t + 1) * 128]
            line += 1
    v1 = remote(small, small1, m_send.at[0], m_recv.at[0], sibling)
    v2 = remote(small, small2, m_send.at[1], m_recv.at[1], across_y)

    def v3(t):
        return remote(small, small3.at[t - 1], m_send.at[1 + t], m_recv.at[1 + t], along[t - 1])

    v1.start()
    v1.wait()
    small[...] += small1[...]
    v2.start()
    ready = set()
    for p, (rows, cols, t, at) in enumerate(plan):
        if t not in ready:
            ready.add(t)
            for load in loads[t]:
                load.wait()
        piece(left_buf[t], right_buf[t], at, cols, buf1[p])
        for yy in range(2):
            first(p, yy).start()
        if p > 0:
            reduce_core(p - 1)
        if p == 1:
            v2.wait()
            small[...] += small2[...]
            for t in range(1, 4):
                v3(t).start()
    reduce_core(count - 1)
    for t, zz in enumerate((seq, far_z)):
        back_near(t).wait_recv()
        back_add(back_rows(zz), back_rec[t])
    back_far().start()
    for load in ffn_loads:
        load.wait()
    ffn_buf[0, ffn_half(1 - y), :] = ffn_sum(1 - y).astype(BF16)
    ffn_sent().start()
    for p in range(count):
        reduce_y(p)
        if p > 0:
            reduce_next(p - 1)
    reduce_next(count - 1)
    own = ffn_sum(y)
    ffn_sent().wait_recv()
    ffn_out[...] = own + ffn_rec[...].astype(F32)
    back_far().wait_recv()
    back_out[...] = back_buf[0, back_rows(seq), :].astype(F32) + back_rec[2].astype(F32)
    for t in range(1, 4):
        v3(t).wait()
    small_out[...] = small[...] + small3[0] + small3[1] + small3[2]
    for p in range(count):
        reduce_far(p)

    for p in range(count):
        for yy in range(2):
            first(p, yy).wait_send()
        second(p).wait_send()
        for t in range(2):
            third(p, t).wait_send()
        fourth(p).wait_send()
    @pl.loop(0, steps)
    def _(i):
        to_tokens.wait_sent(i)

    ffn_sent().wait_send()
    for t in range(2):
        back_near(t).wait_send()
    back_far().wait_send()
    blocks.wait()


def grads_call(d_parts, dr, x, w, g1, att_t, norm_t, d_proj, ffn, back, sums, each):
    width, tokens = att_t.shape
    plan = attn_plan(width)
    count = len(plan)
    steps = tokens // TOK
    one = sds((8, width), F32)
    lines = (4 * width + sum(s.shape[1] for s in sums)) // 128
    vec = pltpu.VMEM((lines, 128), F32)
    buf = lambda s: pltpu.VMEM(s.shape, s.dtype)
    half = (ffn[0].shape[0] // 2, ffn[0].shape[1])
    quarter = (back[0].shape[0] // 4, back[0].shape[1])
    return pl.pallas_call(
        partial(grads_kernel, len(sums)),
        in_specs=[ANY] * 6 + [VMEM] + [ANY] * 9 + [VMEM] * len(sums),
        out_specs=[VMEM] * 5 + [ANY],
        out_shape=[sds((width // 16, width), F32), sds((width // 16, 3 * width), F32)]
        + [sds(half, F32), sds(quarter, F32)]
        + [sds((lines, 128), F32), sds((each, tokens // each, width), BF16)],
        scratch_shapes=(
            [buf(att_t), buf(norm_t), buf(d_proj), pltpu.VMEM((tokens, 3 * width), BF16), buf(w), buf(dr), buf(x), buf(x)]
            + [buf(one)] * 4
            + [pltpu.VMEM((4,) + ffn[0].shape, BF16), pltpu.VMEM(half, BF16),
               pltpu.VMEM((2,) + back[0].shape, BF16), pltpu.VMEM((3,) + quarter, BF16)]
            + [pltpu.VMEM((r, c), BF16) for r, c, *_ in plan]
            + [pltpu.VMEM((r // 2, c), BF16) for r, c, *_ in plan]
            + [pltpu.VMEM((r // 4, c), BF16) for r, c, *_ in plan]
            + [pltpu.VMEM((3, r // 16, c), BF16) for r, c, *_ in plan]
            + [vec, vec, vec, pltpu.VMEM((3, lines, 128), F32)]
            + [DMA((2, 2)), DMA((count, 2)), DMA((count, 2)), DMA((count,)), DMA((count,)),
               DMA((count, 3)), DMA((count, 3)), DMA((5,)), DMA((5,)), DMA, DMA, DMA((4,)), DMA((2,)), DMA((3,)), DMA((3,)),
               DMA((2, steps))]
            + swap_sems(3, steps) + [DMA, DMA((each,)), DMA((each,))]),
        compiler_params=pltpu.CompilerParams(collective_id=8, has_side_effects=True, vmem_limit_bytes=62 * MIB),
        name="weight_grads",
    )(*d_parts, dr, x, w, g1, att_t, norm_t, d_proj, *ffn, *back, *sums)


def finish_kernel(dx_ref, y_ref, *refs):
    count = (len(refs) - 2) // 2
    ins, (dx_out, y_out), outs = refs[:count], refs[count:count + 2], refs[count + 2:]
    dx_out[...] = dx_ref[...].astype(F32)
    y_out[...] = y_ref[...]

    @pl.when(pl.program_id(0) == 0)
    def _():
        for a, b in zip(ins, outs):
            b[...] = a[...]


def finish_call(dx, y, *arrays):
    each, local, width = dx.shape
    block = pl.BlockSpec((1, local // 2, width), lambda i: (i // 2, i % 2, 0))
    whole = [pl.BlockSpec(a.shape, lambda i: (0, 0)) for a in arrays]
    return pl.pallas_call(
        finish_kernel,
        grid=(2 * each,),
        in_specs=[block, block] + whole,
        out_specs=[block, block] + whole,
        out_shape=[sds(dx.shape, F32), sds(y.shape, y.dtype)] + [sds(a.shape, a.dtype) for a in arrays],
        compiler_params=pltpu.CompilerParams(vmem_limit_bytes=62 * MIB),
        name="finish",
    )(dx, y, *arrays)


def swap_cores(x):
    size = lax.axis_size("dp")
    return lax.ppermute(x, "dp", [(i, i ^ 1) for i in range(size)])


def swap_y(x):
    size = lax.axis_size("dp")
    return lax.ppermute(x, "dp", [(i, i ^ 2) for i in range(size)])


def along_seq(x, by):
    size = lax.axis_size("seq")
    return lax.ppermute(x, "seq", [(i, (i + by) % size) for i in range(size)])


def on_device_rows(cell_tokens, cell_lengths, out_grad, *raw_weights):
    (gain1, bias1, wqkv, qb, vb, wo, bo, gain2, bias2, win, bi, wback, bb) = tuple(
        (w if w.ndim == 2 else w[0] for w in raw_weights)
    )
    each, local, width = cell_tokens.shape
    row_length = local * lax.axis_size("seq")
    core = lax.axis_index("dp") % 2
    z = lax.axis_index("seq")

    lengths = jnp.where(z // each == core, cell_lengths, swap_cores(cell_lengths))
    lengths = lax.dynamic_index_in_dim(lengths, z % each, 0, keepdims=False)
    fq, fk, lo, hi = segment_terms(lengths, row_length)

    x, q, k, v = first_call(cell_tokens, wqkv, gain1, bias1, qb, vb)
    o, _ = attn_fwd(lo, hi, q, k, v, fq, fk)
    x, g, norm_t, q, k, v = pass_call(
        o, x, out_grad, wo, win, wback, wqkv, (bo, gain2, bias2, bi, bb, gain1, bias1, qb, vb))
    o, lse = attn_fwd(lo, hi, q, k, v, fq, fk)
    y, resid, slope, att_t, c_t, act_t, dr, do = turn_call(o, x, g, wo, win, wback, (bo, gain2, bias2, bi, bb))

    dq, dk, dv = attn_bwd(lo, hi, q, k, v, do, o, lse, fq, fk)
    outputs, dr, dp, do, *rest = back_call(
        dq, dk, dv, dr, x, y, g, slope, resid, c_t, act_t, wqkv, wo, win, wback, gain1, gain2, each)
    ffn = [w if t == 0 else along_seq(w, t) for t, w in enumerate(rest[:4])]
    back = [rest[4], swap_y(rest[5])]
    s_gain2, s_bias2, s_out, s_in, s_back = rest[6:]
    dq, dk, dv = attn_bwd(lo, hi, q, k, v, do, o, lse, fq, fk)
    sums = (s_out, s_gain2, s_bias2, s_in, s_back)
    g_out, g_qkv, g_in, g_back, small, in_grads = grads_call(
        (dq, dk, dv), dr, x, wqkv, gain1, att_t, norm_t, dp, ffn, back, sums, each)
    in_grads, outputs, g_out, g_qkv, g_in, g_back = finish_call(in_grads, outputs, g_out, g_qkv, g_in, g_back)

    flat = small.reshape(-1)
    parts = lax.axis_size("dp") * lax.axis_size("seq")
    owner = lax.axis_index("dp") * lax.axis_size("seq") + z
    shares, at = [], 0
    for total in [width] * 4 + [s.shape[1] for s in sums]:
        size = total // parts
        shares.append(lax.dynamic_slice_in_dim(flat, at + owner * size, size))
        at += total
    return (
        outputs[None],
        in_grads[None],
        shares[0][None],
        shares[1][None],
        g_qkv[None],
        shares[2][None],
        shares[3][None],
        g_out[None],
        shares[4][None],
        shares[5][None],
        shares[6][None],
        g_in[None],
        shares[7][None],
        g_back[None],
        shares[8][None],
    )


def either_plan(cell_tokens, *others):
    one_chip = lax.axis_size("dp") % 2 == 0 and lax.axis_size("seq") == 2 * cell_tokens.shape[0] and lax.axis_size("section") == 2 and lax.axis_size("dp") == lax.axis_size("seq") == 4
    return (on_device_rows if one_chip else on_device)(cell_tokens, *others)


def solution(mesh):
    in_specs = (
        P("dp", "seq", None),
        P("dp", None),
        P("dp", "seq", None),
        P("section", None),
        P("section", None),
        P("section", None, None),
        P("section", None),
        P("section", None),
        P("section", None, None),
        P("section", None),
        P("section", None),
        P("section", None),
        P("section", None, None),
        P("section", None),
        P("section", None, None),
        P("section", None),
    )
    out_specs = (
        P("section", "dp", "seq", None),
        P("section", "dp", "seq", None),
        P("section", ("dp", "seq")),
        P("section", ("dp", "seq")),
        P("section", ("dp", "seq"), None),
        P("section", ("dp", "seq")),
        P("section", ("dp", "seq")),
        P("section", ("dp", "seq"), None),
        P("section", ("dp", "seq")),
        P("section", ("dp", "seq")),
        P("section", ("dp", "seq")),
        P("section", ("dp", "seq"), None),
        P("section", ("dp", "seq")),
        P("section", ("dp", "seq"), None),
        P("section", ("dp", "seq")),
    )
    return jax.shard_map(
        either_plan, mesh=mesh, in_specs=in_specs, out_specs=out_specs, check_vma=False
    )
```

profile of v0, /device:TPU:0, one launch (start us, length us, event | category | flops | bytes accessed | tf_op | source)
XLA Modules:
  0.0 470.4 jit_solution(1974151868732118103)
XLA Ops:
  0.6 0.5 collective-permute-start
  1.2 0.0 copy-start.2
  1.2 30.6 %rows_qkv.1 = (bf16[1024,768]{1,0:T(8,128)(2,1)}, bf16[2048,384]{1,0:T(8,128)(2,1)}, bf16[2048,384]{1,0:T(8,128)(2,1)}, bf16[2048,384]{1,0:T(8,128)(2,1)}) custom-call(bf16[2,512,768]{2,1,0:T(8,128)(2,1)} %x_ref.1, bf16[768,2304]{1,0:T(8,128)(2,1)} %bitcast.38, bf16[1,768]{1,0:T(2,128)(2,1)} %refs_6_.1, bf16[1,768]{1,0:T(2,128)(2,1)} %b1.1, ...), custom_call_target="tpu_custom_call" | custom-call | tf_op jit(solution)/shard_map/rows_qkv/pallas_call | solution.py:871
  31.8 0.0 collective-permute-done
  31.9 0.0 copy-done.2
  31.9 0.1 select_reduce_fusion
  32.0 0.2 select_reduce_fusion.1
  32.2 0.2 select_reduce_fusion.2
  32.4 0.5 and_select_fusion
  32.9 1.3 select_convert_fusion
  34.3 19.1 %attn_fwd.2 = (bf16[2048,384]{1,0:T(8,128)(2,1)}, f32[3,8,2048]{2,1,0:T(8,128)}) custom-call(s32[8]{0:T(128)} %get-tuple-element.134.lo_ref, s32[8]{0:T(128)} %get-tuple-element.133.hi_ref, bf16[2048,384]{1,0:T(8,128)(2,1)} %get-tuple-element.69.q_ref, bf16[2048,384]{1,0:T(8,128)(2,1)} %get-tuple-element.70.k_ref, ...), custom_call_target="tpu_custom_call" | custom-call | tf_op jit(solution)/shard_map/attn_fwd/pallas_call | solution.py:417
  53.4 60.8 %ffn_pass_qkv.1 = (bf16[1024,768]{1,0:T(8,128)(2,1)}, bf16[1024,768]{1,0:T(8,128)(2,1)}, bf16[768,1024]{1,0:T(8,128)(2,1)}, bf16[2048,384]{1,0:T(8,128)(2,1)}, b...) custom-call(bf16[2048,384]{1,0:T(8,128)(2,1)} %get-tuple-element.72.o_ref, ...), custom_call_target="tpu_custom_call" | custom-call | tf_op jit(solution)/shard_map/ffn_pass_qkv/pallas_call | solution.py:1051
  114.2 19.0 %attn_fwd.3 = (bf16[2048,384]{1,0:T(8,128)(2,1)}, f32[3,8,2048]{2,1,0:T(8,128)}) custom-call(s32[8]{0:T(128)} %get-tuple-element.134.lo_ref, s32[8]{0:T(128)} %get-tuple-element.133.hi_ref, bf16[2048,384]{1,0:T(8,128)(2,1)} %get-tuple-element.74.q_ref, bf16[2048,384]{1,0:T(8,128)(2,1)} %get-tuple-element.75.k_ref, ...), custom_call_target="tpu_custom_call" | custom-call | tf_op jit(solution)/shard_map/attn_fwd/pallas_call | solution.py:417
  133.2 42.9 %ffn_turn.1 = (bf16[1024,768]{1,0:T(8,128)(2,1)}, f32[1024,768]{1,0:T(8,128)}, bf16[1024,3072]{1,0:T(8,128)(2,1)}, bf16[768,1024]{1,0:T(8,128)(2,1)}, bf16[768,1...) custom-call(bf16[2048,384]{1,0:T(8,128)(2,1)} %get-tuple-element.77.o_ref, ...), custom_call_target="tpu_custom_call" | custom-call | tf_op jit(solution)/shard_map/ffn_turn/pallas_call | solution.py:1138
  176.0 32.3 %attn_bwd.2 = (bf16[2048,384]{1,0:T(8,128)(2,1)}, bf16[2048,384]{1,0:T(8,128)(2,1)}, bf16[2048,384]{1,0:T(8,128)(2,1)}) custom-call(s32[8]{0:T(128)} %get-tuple-element.134.lo_ref, s32[8]{0:T(128)} %get-tuple-element.133.hi_ref, bf16[2048,384]{1,0:T(8,128)(2,1)} %get-tuple-element.74.q_ref, bf16[2048,384]{1,0:T(8,128)(2,1)} %get-tuple-element.75.k_ref, ...), custom_call_target="tpu_custom_call" | custom-call | tf_op jit(solution)/shard_map/attn_bwd/pallas_call | solution.py:523
  208.3 106.3 %qkv_back_pass.1 = (bf16[2,512,768]{2,1,0:T(8,128)(2,1)}, f32[1024,768]{1,0:T(8,128)}, bf16[1024,768]{1,0:T(8,128)(2,1)}, bf16[2048,384]{1,0:T(8,128)(2,1)}, bf1...) custom-call(bf16[2048,384]{1,0:T(8,128)(2,1)} %get-tuple-element.82., ...), custom_call_target="tpu_custom_call" | custom-call | tf_op jit(solution)/shard_map/qkv_back_pass/pallas_call | solution.py:1371
  314.6 0.1 collective-permute-start.4
  314.6 0.7 collective-permute-start.1
  315.3 0.1 collective-permute-start.2
  315.4 3.1 collective-permute-start.3
  318.5 32.2 %attn_bwd.3 = (bf16[2048,384]{1,0:T(8,128)(2,1)}, bf16[2048,384]{1,0:T(8,128)(2,1)}, bf16[2048,384]{1,0:T(8,128)(2,1)}) custom-call(s32[8]{0:T(128)} %get-tuple-element.134.lo_ref, s32[8]{0:T(128)} %get-tuple-element.133.hi_ref, bf16[2048,384]{1,0:T(8,128)(2,1)} %get-tuple-element.74.q_ref, bf16[2048,384]{1,0:T(8,128)(2,1)} %get-tuple-element.75.k_ref, ...), custom_call_target="tpu_custom_call" | custom-call | tf_op jit(solution)/shard_map/attn_bwd/pallas_call | solution.py:523
  350.8 0.0 collective-permute-done.1.refs_11_
  350.8 0.0 copy-start.1
  350.8 5.9 %collective-permute-done.2.refs_12_ = bf16[96,3072]{1,0:T(8,128)(2,1)} collective-permute-done((bf16[96,3072]{1,0:T(8,128)(2,1)}, bf16[96,3072]{1,0:T(8,128)(2,1)}, u32[]{:S(2)}, u32[]{:S(2)}) %collective-permute-start.2) | collective-permute-done | bytes 589856 | tf_op jit(solution)/shard_map/ppermute | solution.py:1721
  356.7 0.0 collective-permute-done.3.refs_13_
  356.7 0.0 collective-permute-done.4.refs_15_
  356.7 0.0 copy-done.1
  356.7 1.0 copy-done
  357.7 103.8 %weight_grads.1 = (f32[48,768]{1,0:T(8,128)}, f32[48,2304]{1,0:T(8,128)}, f32[48,3072]{1,0:T(8,128)}, f32[192,768]{1,0:T(8,128)}, f32[72,128]{1,0:T(8,128)}, /*index=5*/bf16[2,512,768]{2,1,0:T(8,128)(2,1)}) custom-call(bf16[2048,384]{1,0:T(8,128)(2,1)} %get-tuple-element.92.refs_0_, bf16[2048,384]{1,0:T(8,128)(2,1)} %get-tuple-element.93.refs_1_, ...), custom_call_target="tpu_custom_call" | custom-call | tf_op jit(solution)/shard_map/weight_grads/pallas_call | solution.py:1656
  461.5 1.3 dynamic_slice.39
  462.9 5.8 %finish.1 = (f32[2,512,768]{2,1,0:T(8,128)}, bf16[2,512,768]{2,1,0:T(8,128)(2,1)}, f32[48,768]{1,0:T(8,128)}, f32[48,2304]{1,0:T(8,128)}, f32[48,3072]{1,0:T(8,128)}, /*index=5*/f32[192,768]{1,0:T(8,128)}) custom-call(bf16[2,512,768]{2,1,0:T(8,128)(2,1)} %get-tuple-element.110.dx_ref, bf16[2,512,768]{2,1,0:T(8,128)(2,1)} %get-tuple-element.111.y_ref, ...), custom_call_target="tpu_custom_call" | custom-call | tf_op jit(solution)/shard_map/finish/pallas_call | solution.py:1698
  468.7 1.5 dynamic-slice_bitcast_fusion
  (10 shorter events, 0.1 us)
Async XLA Ops:
  0.6 31.2 %collective-permute-start = (s32[2,16]{1,0:T(2,128)}, s32[2,16]{1,0:T(2,128)S(1)}, u32[]{:S(2)}, u32[]{:S(2)}) collective-permute-start(s32[2,16]{1,0:T(2,128)} %param.17), channel_id=1, source_target_pairs={{0,4},{4,0},{8,12},{12,8},{1,5},{5,1},{9,13},{13,9},{2,6},{6,2},{1... | collective-permute-start | bytes 392 | tf_op jit(solution)/shard_map/ppermute | solution.py:1711
  1.2 30.6 %copy-start.2 = (s32[2,16]{1,0:T(2,128)S(1)}, s32[2,16]{1,0:T(2,128)}, u32[]{:S(2)}) copy-start(s32[2,16]{1,0:T(2,128)} %param.17) | copy-start | bytes 388
  314.6 42.2 %collective-permute-start.4 = (bf16[768,768]{1,0:T(8,128)(2,1)}, bf16[768,768]{1,0:T(8,128)(2,1)S(1)}, u32[]{:S(2)}, u32[]{:S(2)}) collective-permute-start(bf16[768,768]{1,0:T(8,128)(2,1)} %get-tuple-element.104), channel_id=1, source_target_pairs={{0,8},{4,12},{8,0},{12,4},{1,9},{5,13},{9,1},{13,5},{2,10},{6,14},... | collective-permute-start | bytes 3538952 | tf_op jit(solution)/shard_map/ppermute | solution.py:1716
  314.6 36.1 %collective-permute-start.1 = (bf16[96,3072]{1,0:T(8,128)(2,1)}, bf16[96,3072]{1,0:T(8,128)(2,1)S(1)}, u32[]{:S(2)}, u32[]{:S(2)}) collective-permute-start(bf16[96,3072]{1,0:T(8,128)(2,1)} %get-tuple-element.100), channel_id=1, source_target_pairs={{0,1},{1,2},{2,3},{3,0},{4,5},{5,6},{6,7},{7,4},{8,9},{9,10},{10,1... | collective-permute-start | bytes 1769480 | tf_op jit(solution)/shard_map/ppermute | solution.py:1721
  315.3 41.4 %collective-permute-start.2 = (bf16[96,3072]{1,0:T(8,128)(2,1)}, bf16[96,3072]{1,0:T(8,128)(2,1)}, u32[]{:S(2)}, u32[]{:S(2)}) collective-permute-start(bf16[96,3072]{1,0:T(8,128)(2,1)} %get-tuple-element.101), channel_id=1, source_target_pairs={{0,2},{1,3},{2,0},{3,1},{4,6},{5,7},{6,4},{7,5},{8,10},{9,11},{10,... | collective-permute-start | bytes 1769480 | tf_op jit(solution)/shard_map/ppermute | solution.py:1721
  315.4 41.3 %collective-permute-start.3 = (bf16[96,3072]{1,0:T(8,128)(2,1)}, bf16[96,3072]{1,0:T(8,128)(2,1)}, u32[]{:S(2)}, u32[]{:S(2)}) collective-permute-start(bf16[96,3072]{1,0:T(8,128)(2,1)} %get-tuple-element.102), channel_id=1, source_target_pairs={{0,3},{1,0},{2,1},{3,2},{4,7},{5,4},{6,5},{7,6},{8,11},{9,8},{10,9... | collective-permute-start | bytes 1769480 | tf_op jit(solution)/shard_map/ppermute | solution.py:1721
  350.8 6.0 %copy-start.1 = (bf16[96,3072]{1,0:T(8,128)(2,1)}, bf16[96,3072]{1,0:T(8,128)(2,1)S(1)}, u32[]{:S(2)}) copy-start(bf16[96,3072]{1,0:T(8,128)(2,1)S(1)} %collective-permute-done.1.refs_11_) | copy-start | bytes 1769476
  356.7 1.0 copy-start
where the time goes:
time: 475 us; the launch traced here: 470 us
  Pallas kernels  453 us (95%)
  waiting for transfers between devices  5.94 us (1%)
    pallas_call x1, Pallas kernels, back_call(): pl.pallas_call(back_kernel, in_specs=[ANY] * 15 + [VMEM, VMEM], out_specs...  106 us
    pallas_call x1, Pallas kernels, grads_call(): pl.pallas_call(partial(grads_kernel, len(sums)), in_specs=[ANY] * 6 + [VM...  104 us
    pallas_call x2, Pallas kernels, attn_bwd(): pl.pallas_call(bwd_kernel, grid_spec=pltpu.PrefetchScalarGridSpec(num_sca...  64.5 us
    pallas_call x1, Pallas kernels, pass_call(): pl.pallas_call(pass_kernel, in_specs=[ANY, VMEM, ANY, ANY, ANY, ANY, ANY]...  60.8 us
    pallas_call x1, Pallas kernels, turn_call(): pl.pallas_call(turn_kernel, in_specs=[ANY, VMEM, VMEM, ANY, ANY, ANY] + [...  42.9 us
    pallas_call x2, Pallas kernels, attn_fwd(): pl.pallas_call(fwd_kernel, grid_spec=pltpu.PrefetchScalarGridSpec(num_sca...  38.1 us
    pallas_call x1, Pallas kernels, first_call(): pl.pallas_call(first_kernel, in_specs=[ANY, ANY] + [VMEM] * 4, out_specs=...  30.6 us
  transfers between devices with their start and end apart: 5, of which 1 were waited for; matrix products, arithmetic and copies ran while one was open for 0% of the time, Pallas kernels for 13%

commit v1 on v0

--- a/solution.py
+++ b/solution.py
@@ -1062,8 +1062,13 @@
     )(o, x, g, wo, win, wback, wqkv, *vectors)
 
 
-def turn_kernel(o_ref, x_ref, g_ref, wo_in, win_in, wback_in, bo, g2, b2, bi, bb,
-                y_out, resid_out, slope_out, att_out, c_out, act_out, dr_out, da_ref,
+def turn_kernel(each, o_ref, x_ref, g_ref, wo_in, win_in, wback_in, bo, g2, b2, bi, bb, *refs):
+    y_outs, refs = refs[:each], refs[each:]
+    turn_body(each, y_outs, o_ref, x_ref, g_ref, wo_in, win_in, wback_in, bo, g2, b2, bi, bb, *refs)
+
+
+def turn_body(each, y_outs, o_ref, x_ref, g_ref, wo_in, win_in, wback_in, bo, g2, b2, bi, bb,
+                resid_out, slope_out, att_out, c_out, act_out, dr_out, da_ref,
                 wo, win, wback, att, yb, resid_b, slope_b, att_t, c_t, act_t, dr_b, da_b,
                 w_sem, out_sem, *sems):
     section, dp, seq, core = place()
@@ -1087,8 +1092,16 @@
         where = (slice(None), chunk(i)) if turned else (chunk(i),)
         return [pltpu.make_async_copy(b.at[where], o.at[where], out_sem.at[at + n, i]) for n, (b, o) in enumerate(which)]
 
+    def y_moves(i, act):
+        per = tokens // each // TOK
+        step = lax.rem(seq - i // per + each, each)
+        for n in range(each):
+            @pl.when(step == n)
+            def _():
+                act(pltpu.make_async_copy(yb.at[chunk(i)], y_outs[n].at[chunk(lax.rem(i, per))], out_sem.at[0, i]))
+
     def results(i):
-        return copies(i, ((yb, y_out), (resid_b, resid_out), (slope_b, slope_out)), 0) + copies(
+        return copies(i, ((resid_b, resid_out), (slope_b, slope_out)), 1) + copies(
             i, ((att_t, att_out), (c_t, c_out), (act_t, act_out)), 3, True)
 
     def back_results(i):
@@ -1102,6 +1115,7 @@
 
     to_tokens.wait(0)
     in_turns(forward(0, loads))
+    y_moves(jnp.int32(0), lambda copy: copy.start())
     for copy in results(0):
         copy.start()
 
@@ -1111,6 +1125,7 @@
         in_turns(forward(i))
         in_turns(backward(i - 1))
         to_heads.start(i - 1)
+        y_moves(i, lambda copy: copy.start())
         for copy in results(i) + back_results(i - 1):
             copy.start()
 
@@ -1123,24 +1138,25 @@
     def _(i):
         to_tokens.wait_sent(i)
         to_heads.wait(i)
+        y_moves(i, lambda copy: copy.wait())
         for copy in results(i) + back_results(i):
             copy.wait()
 
 
-def turn_call(o, x, g, wo, win, wback, vectors):
+def turn_call(o, x, g, wo, win, wback, vectors, each):
     tokens, width = x.shape
     hidden = win.shape[1]
     steps = tokens // TOK
     low, full = sds(x.shape, BF16), sds(x.shape, F32)
     turned = sds((width, tokens), BF16)
-    outs = [low, full, sds((tokens, hidden), BF16), turned, turned, sds((hidden, tokens), BF16), full]
+    outs = [full, sds((tokens, hidden), BF16), turned, turned, sds((hidden, tokens), BF16), full]
     buf = lambda s: pltpu.VMEM(s.shape, s.dtype)
     return pl.pallas_call(
-        turn_kernel,
+        partial(turn_kernel, each),
         in_specs=[ANY, VMEM, VMEM, ANY, ANY, ANY] + [VMEM] * len(vectors),
-        out_specs=[ANY] * 8,
-        out_shape=outs + [sds((2 * tokens, width // 2), BF16)],
-        scratch_shapes=[buf(wo), buf(win), buf(wback), buf(low)] + [buf(s) for s in outs] + [buf(low)]
+        out_specs=[ANY] * (each + 7),
+        out_shape=[sds((tokens // each, width), BF16)] * each + outs + [sds((2 * tokens, width // 2), BF16)],
+        scratch_shapes=[buf(wo), buf(win), buf(wback), buf(low), buf(low)] + [buf(s) for s in outs] + [buf(low)]
         + [DMA((1 + 2 * (hidden // COLS),)), DMA((7, steps))] + swap_sems(1, steps) + swap_sems(1, steps),
         compiler_params=pltpu.CompilerParams(collective_id=3, has_side_effects=True, vmem_limit_bytes=62 * MIB),
         name="ffn_turn",
@@ -1161,9 +1177,9 @@
     return (dr[rows, :] + row_norm_back(d_a, hat, rstd, up(gain))).astype(BF16)
 
 
-def back_kernel(dq_ref, dk_ref, dv_ref, dr_ref, x_ref, y_ref, g_in, slope_in, resid_in, c_in, act_in,
+def back_kernel(dq_ref, dk_ref, dv_ref, dr_ref, x_ref, g_in, slope_in, resid_in, c_in, act_in,
                 wqkv_in, wo_in, win_in, wback_in, g1, g2,
-                y_out, dr_out, dp_out, da_ref, *rest):
+                dx_out, dr_out, dp_out, da_ref, *rest):
     rest = list(rest)
     shares = [rest.pop(0) for _ in range(4)]
     y_shares = [rest.pop(0) for _ in range(2)]
@@ -1210,7 +1226,7 @@
     greet(across, *column_mates(section, dp_index, seq, core))
     to_tokens = ToTokens((dq_ref, dk_ref, dv_ref), dj, tokens, width, sems[:3], core, sibling)
     to_heads = ToHeads(da_b, (da_ref,), tokens, width, sems[3:6], core, sibling)
-    blocks = Blocks(y_ref, y_out, False, sems[6:10], section, dp_index, seq, core)
+    own_blocks = Blocks(dx, dx_out, False, [None] + sems[6:9], section, dp_index, seq, core)
 
     @pl.when(section == 1)
     def _():
@@ -1231,6 +1247,8 @@
             dx[chunk(i), :] = input_back(i, dj, dr_in, x_b, wqkv, g1, None)
             passed(i).start()
 
+        own_blocks.start()
+
     for load in loads[1:]:
         load.start()
 
@@ -1241,7 +1259,6 @@
 
     for i in range(2):
         turned(i).start()
-    blocks.start()
     sums = (s_gain, s_bias, s_out, s_in, s_back)
     for s in sums + (grad_in, grad_back):
         s[...] = jnp.zeros_like(s)
@@ -1356,10 +1373,13 @@
         write_back(yy).wait()
         for t in range(4):
             write_in(t, yy).wait()
-    blocks.wait()
-
-
-def back_call(dq, dk, dv, dr, x, y, g, slope, resid, c_t, act_t, wqkv, wo, win, wback, g1, g2, each):
+
+    @pl.when(section == 1)
+    def _():
+        own_blocks.wait()
+
+
+def back_call(dq, dk, dv, dr, x, g, slope, resid, c_t, act_t, wqkv, wo, win, wback, g1, g2, each):
     tokens, width = x.shape
     hidden = win.shape[1]
     steps = tokens // TOK
@@ -1370,7 +1390,7 @@
     shares = [sds((width // 8, hidden), BF16)] * 4 + [sds((hidden // 4, width), BF16)] * 2
     return pl.pallas_call(
         back_kernel,
-        in_specs=[ANY] * 15 + [VMEM, VMEM],
+        in_specs=[ANY] * 14 + [VMEM, VMEM],
         out_specs=[ANY] * 10 + [VMEM] * 5,
         out_shape=[sds((each, tokens // each, width), BF16), full, low, sds((2 * tokens, width // 2), BF16)]
         + shares + [one, one, one, sds((8, hidden), F32), one],
@@ -1380,10 +1400,10 @@
                         DMA((5,)), DMA((2, steps)), DMA((2, steps)), DMA((steps,)), DMA((2, steps)), DMA((steps,)),
                         DMA((steps,)), DMA((steps,)), pltpu.SemaphoreType.REGULAR,
                         DMA((2 * blocks_of + 2,)), DMA((2 * blocks_of + 2,)), DMA((5, 2))]
-        + swap_sems(3, steps) + swap_sems(1, steps) + block_scratch(each, tokens // each, width),
+        + swap_sems(3, steps) + swap_sems(1, steps) + block_scratch(each, 16, width)[1:],
         compiler_params=pltpu.CompilerParams(collective_id=4, has_side_effects=True, vmem_limit_bytes=62 * MIB),
         name="qkv_back_pass",
-    )(dq, dk, dv, dr, x, y, g, slope, resid, c_t, act_t, wqkv, wo, win, wback, g1, g2)
+    )(dq, dk, dv, dr, x, g, slope, resid, c_t, act_t, wqkv, wo, win, wback, g1, g2)
 
 
 def core_rows(size, yy, core):
@@ -1406,6 +1426,8 @@
 def grads_kernel(n_small, *refs):
     refs = list(refs)
     d_parts = [refs.pop(0) for _ in range(3)]
+    d_early = [refs.pop(0) for _ in range(3)]
+    dx_early = refs.pop(0)
     dr_ref, x_ref, w_in, g1 = [refs.pop(0) for _ in range(4)]
     lefts = [refs.pop(0) for _ in range(2)]
     rights = [refs.pop(0)]
@@ -1430,6 +1452,7 @@
     small, small1, small2, small3 = [refs.pop(0) for _ in range(4)]
     (load_sem, s1_send, s1_recv, s2_send, s2_recv, s3_send, s3_recv,
      m_send, m_recv, f_send, f_recv, f_load, b_load, b_send, b_recv, in_sem) = refs[:16]
+    relay, way_send, way_recv, on_send, on_recv, e_sem = refs[22:]
 
     section, dp, seq, core = place()
     y = dp // 2
@@ -1447,9 +1470,95 @@
         return [pltpu.make_async_copy(a.at[chunk(i)], b.at[chunk(i)], in_sem.at[n, i])
                 for n, (a, b) in enumerate(((x_ref, x), (dr_ref, dr)))]
 
-    greet(across_y, *column_mates(section, dp, seq, core))
+    column = dp - core
+    across = (1 - section, dp, seq)
+    each, local, _ = dx_out.shape
+    part = local // 2
+    mates = [across_y] + column_mates(section, dp, seq, core)
+    barrier = pltpu.get_barrier_semaphore()
+    for mate in mates:
+        pl.semaphore_signal(barrier, 1, device_id=mate, device_id_type=MESH)
+
+    @pl.when(section == 1)
+    def _():
+        pl.semaphore_signal(barrier, 1, device_id=across, device_id_type=MESH)
+
+    pl.semaphore_wait(barrier, len(mates) + 1 - section)
     to_tokens = ToTokens(d_parts, dj, tokens, width, refs[16:19], core, sibling)
-    blocks = Blocks(dxb, dx_out, False, [None] + refs[19:22], section, dp, seq, core)
+    to_tokens_early = ToTokens(d_early, dj, tokens, width, refs[16:19], core, sibling)
+    own_sem, way0_send, way0_recv = refs[19:22]
+
+    def goal(j):
+        target_core, target_seq = seq // each, core * each + j
+        here = (target_core == core) & (target_seq == seq)
+        return here, lax.rem(seq, each), (0, column + target_core, target_seq)
+
+    def straight(j):
+        _, slot, target = goal(j)
+        return remote(dxb.at[pl.ds(j * local, part)], dx_out.at[slot, pl.ds(0, part)], way0_send.at[j], way0_recv.at[slot], target)
+
+    def detour(j):
+        return remote(dxb.at[pl.ds(j * local + part, part)], relay.at[j], way_send.at[j], way_recv.at[j], across)
+
+    def onward(j):
+        _, slot, target = goal(j)
+        return remote(relay.at[j], dx_out.at[slot, pl.ds(part, part)], on_send.at[j], on_recv.at[slot], target)
+
+    def stay(j):
+        return pltpu.make_async_copy(dxb.at[pl.ds(j * local, local)], dx_out.at[lax.rem(seq, each)], own_sem)
+
+    def dx_start(j):
+        here = goal(j)[0]
+
+        @pl.when((section == 0) & here)
+        def _():
+            stay(j).start()
+
+        @pl.when((section == 0) & jnp.logical_not(here))
+        def _():
+            straight(j).start()
+            detour(j).start()
+
+    def dx_forward(j):
+        @pl.when((section == 1) & jnp.logical_not(goal(j)[0]))
+        def _():
+            detour(j).wait_recv()
+            onward(j).start()
+
+    def dx_finish():
+        for j in range(each):
+            here = goal(j)[0]
+
+            @pl.when((section == 0) & here)
+            def _():
+                stay(j).wait()
+
+            @pl.when((section == 0) & jnp.logical_not(here))
+            def _():
+                straight(j).wait_send()
+                detour(j).wait_send()
+
+            @pl.when((section == 1) & jnp.logical_not(here))
+            def _():
+                onward(j).wait_send()
+        for m in range(each):
+            here = (seq // each == core) & (core * each + m == seq)
+
+            @pl.when((section == 0) & jnp.logical_not(here))
+            def _():
+                remote(dxb.at[pl.ds(0, part)], dx_out.at[m, pl.ds(0, part)], way0_send.at[0], way0_recv.at[m], sibling).wait_recv()
+                remote(relay.at[0], dx_out.at[m, pl.ds(part, part)], on_send.at[0], on_recv.at[m], sibling).wait_recv()
+
+        @pl.when(section == 1)
+        def _():
+            for j in range(each):
+                load = pltpu.make_async_copy(dx_early.at[j], dxb.at[pl.ds(j * local, local)], e_sem.at[0, j])
+                load.start()
+                load.wait()
+                store = pltpu.make_async_copy(dxb.at[pl.ds(j * local, local)], dx_out.at[j], e_sem.at[1, j])
+                store.start()
+                store.wait()
+
     ffn_loads = [pltpu.make_async_copy(ffn_in[t], ffn_buf.at[t], f_load.at[t]) for t in range(4)]
     back_loads = [pltpu.make_async_copy(back_in[t], back_buf.at[t], b_load.at[t]) for t in range(2)]
     for load in back_loads:
@@ -1457,7 +1566,14 @@
 
     @pl.loop(0, steps)
     def _(i):
-        to_tokens.start(i)
+        @pl.when(section == 0)
+        def _():
+            to_tokens.start(i)
+
+        @pl.when(section == 1)
+        def _():
+            to_tokens_early.start(i)
+
         for copy in given(i):
             copy.start()
 
@@ -1565,7 +1681,7 @@
                 copy.wait()
             dxb[chunk(i), :] = input_back(i, dj, dr, x, w, g1, own_sums)
 
-        blocks.start(j)
+        dx_start(j)
 
     line = 0
     for s in own_sums + sums:
@@ -1613,6 +1729,8 @@
         if p > 0:
             reduce_next(p - 1)
     reduce_next(count - 1)
+    for j in range(each):
+        dx_forward(j)
     own = ffn_sum(y)
     ffn_sent().wait_recv()
     ffn_out[...] = own + ffn_rec[...].astype(F32)
@@ -1639,10 +1757,10 @@
     for t in range(2):
         back_near(t).wait_send()
     back_far().wait_send()
-    blocks.wait()
-
-
-def grads_call(d_parts, dr, x, w, g1, att_t, norm_t, d_proj, ffn, back, sums, each):
+    dx_finish()
+
+
+def grads_call(d_parts, d_early, dx_early, dr, x, w, g1, att_t, norm_t, d_proj, ffn, back, sums, each):
     width, tokens = att_t.shape
     plan = attn_plan(width)
     count = len(plan)
@@ -1655,7 +1773,7 @@
     quarter = (back[0].shape[0] // 4, back[0].shape[1])
     return pl.pallas_call(
         partial(grads_kernel, len(sums)),
-        in_specs=[ANY] * 6 + [VMEM] + [ANY] * 9 + [VMEM] * len(sums),
+        in_specs=[ANY] * 10 + [VMEM] + [ANY] * 9 + [VMEM] * len(sums),
         out_specs=[VMEM] * 5 + [ANY],
         out_shape=[sds((width // 16, width), F32), sds((width // 16, 3 * width), F32)]
         + [sds(half, F32), sds(quarter, F32)]
@@ -1673,17 +1791,23 @@
             + [DMA((2, 2)), DMA((count, 2)), DMA((count, 2)), DMA((count,)), DMA((count,)),
                DMA((count, 3)), DMA((count, 3)), DMA((5,)), DMA((5,)), DMA, DMA, DMA((4,)), DMA((2,)), DMA((3,)), DMA((3,)),
                DMA((2, steps))]
-            + swap_sems(3, steps) + [DMA, DMA((each,)), DMA((each,))]),
+            + swap_sems(3, steps) + [DMA, DMA((each,)), DMA((each,))]
+            + [pltpu.VMEM((each, tokens // each // 2, width), BF16)] + [DMA((each,))] * 4 + [DMA((2, each))]),
         compiler_params=pltpu.CompilerParams(collective_id=8, has_side_effects=True, vmem_limit_bytes=62 * MIB),
         name="weight_grads",
-    )(*d_parts, dr, x, w, g1, att_t, norm_t, d_proj, *ffn, *back, *sums)
-
-
-def finish_kernel(dx_ref, y_ref, *refs):
+    )(*d_parts, *d_early, dx_early, dr, x, w, g1, att_t, norm_t, d_proj, *ffn, *back, *sums)
+
+
+def finish_kernel(each, dx_ref, *refs):
+    ys, refs = refs[:each], refs[each:]
     count = (len(refs) - 2) // 2
     ins, (dx_out, y_out), outs = refs[:count], refs[count:count + 2], refs[count + 2:]
     dx_out[...] = dx_ref[...].astype(F32)
-    y_out[...] = y_ref[...]
+    step = lax.rem(pl.program_id(0) // 2 - lax.axis_index("seq") + 4 * each, each)
+    value = ys[0][...]
+    for n in range(1, each):
+        value = jnp.where(step == n, ys[n][...], value)
+    y_out[0] = value
 
     @pl.when(pl.program_id(0) == 0)
     def _():
@@ -1691,24 +1815,38 @@
             b[...] = a[...]
 
 
-def finish_call(dx, y, *arrays):
+def finish_call(dx, ys, *arrays):
     each, local, width = dx.shape
     block = pl.BlockSpec((1, local // 2, width), lambda i: (i // 2, i % 2, 0))
+    half = pl.BlockSpec((local // 2, width), lambda i: (i % 2, 0))
     whole = [pl.BlockSpec(a.shape, lambda i: (0, 0)) for a in arrays]
     return pl.pallas_call(
-        finish_kernel,
+        partial(finish_kernel, each),
         grid=(2 * each,),
-        in_specs=[block, block] + whole,
+        in_specs=[block] + [half] * each + whole,
         out_specs=[block, block] + whole,
-        out_shape=[sds(dx.shape, F32), sds(y.shape, y.dtype)] + [sds(a.shape, a.dtype) for a in arrays],
+        out_shape=[sds(dx.shape, F32), sds(dx.shape, BF16)] + [sds(a.shape, a.dtype) for a in arrays],
         compiler_params=pltpu.CompilerParams(vmem_limit_bytes=62 * MIB),
         name="finish",
-    )(dx, y, *arrays)
+    )(dx, *ys, *arrays)
 
 
 def swap_cores(x):
     size = lax.axis_size("dp")
     return lax.ppermute(x, "dp", [(i, i ^ 1) for i in range(size)])
+
+
+def row_moves(each):
+    n_dp, n_seq = lax.axis_size("dp"), lax.axis_size("seq")
+    steps = []
+    for k in range(each):
+        pairs = []
+        for d in range(n_dp):
+            for z in range(n_seq):
+                source = (2 * (d // 2) + z // each) * n_seq + (d % 2) * each + (z + k) % each
+                pairs.append((source, d * n_seq + z))
+        steps.append(pairs)
+    return steps
 
 
 def swap_y(x):
@@ -1739,19 +1877,23 @@
     x, g, norm_t, q, k, v = pass_call(
         o, x, out_grad, wo, win, wback, wqkv, (bo, gain2, bias2, bi, bb, gain1, bias1, qb, vb))
     o, lse = attn_fwd(lo, hi, q, k, v, fq, fk)
-    y, resid, slope, att_t, c_t, act_t, dr, do = turn_call(o, x, g, wo, win, wback, (bo, gain2, bias2, bi, bb))
+    *ys, resid, slope, att_t, c_t, act_t, dr, do = turn_call(
+        o, x, g, wo, win, wback, (bo, gain2, bias2, bi, bb), each)
+    ys = [lax.ppermute(part, ("dp", "seq"), pairs) for part, pairs in zip(ys, row_moves(each))]
 
     dq, dk, dv = attn_bwd(lo, hi, q, k, v, do, o, lse, fq, fk)
-    outputs, dr, dp, do, *rest = back_call(
-        dq, dk, dv, dr, x, y, g, slope, resid, c_t, act_t, wqkv, wo, win, wback, gain1, gain2, each)
+    dq, *ys = lax.optimization_barrier((dq, *ys))
+    dx_early, dr, dp, do, *rest = back_call(
+        dq, dk, dv, dr, x, g, slope, resid, c_t, act_t, wqkv, wo, win, wback, gain1, gain2, each)
     ffn = [w if t == 0 else along_seq(w, t) for t, w in enumerate(rest[:4])]
     back = [rest[4], swap_y(rest[5])]
     s_gain2, s_bias2, s_out, s_in, s_back = rest[6:]
-    dq, dk, dv = attn_bwd(lo, hi, q, k, v, do, o, lse, fq, fk)
+    hi = jnp.where(lax.axis_index("section") == 1, lo, hi)
+    d_late = attn_bwd(lo, hi, q, k, v, do, o, lse, fq, fk)
     sums = (s_out, s_gain2, s_bias2, s_in, s_back)
     g_out, g_qkv, g_in, g_back, small, in_grads = grads_call(
-        (dq, dk, dv), dr, x, wqkv, gain1, att_t, norm_t, dp, ffn, back, sums, each)
-    in_grads, outputs, g_out, g_qkv, g_in, g_back = finish_call(in_grads, outputs, g_out, g_qkv, g_in, g_back)
+        d_late, (dq, dk, dv), dx_early, dr, x, wqkv, gain1, att_t, norm_t, dp, ffn, back, sums, each)
+    in_grads, outputs, g_out, g_qkv, g_in, g_back = finish_call(in_grads, ys, g_out, g_qkv, g_in, g_back)
 
     flat = small.reshape(-1)
     parts = lax.axis_size("dp") * lax.axis_size("seq")

time: 475 us -> 464 us (0.977)
  Pallas kernels: 453 us -> 426 us
  starting transfers between devices: 4.47 us -> 20.8 us
    pallas_call x4, Pallas kernels: 259 us -> 234 us  [the longest x1 95.8 us: back_call(): pl.pallas_call(back_kernel, in_specs=[ANY] * 14 + [VMEM, VMEM], out_specs...]
    ppermute x0 -> x2, starting transfers between devices: none -> 14.1 us  [on_device_rows(): lax.ppermute(part, ('dp', 'seq'), pairs)]
  transfers between devices with their start and end apart: 5 -> 7, of which waited for: 1 -> 1; matrix products, arithmetic and copies ran while one was open for 0% -> 0% of each run, Pallas kernels for 13% -> 20%
where the time goes in v1:
time: 464 us; the launch traced here: 461 us
  Pallas kernels  426 us (92%)
  starting transfers between devices  20.8 us (4%)
  waiting for transfers between devices  7.75 us (2%)
    pallas_call x1, Pallas kernels, back_call(): pl.pallas_call(back_kernel, in_specs=[ANY] * 14 + [VMEM, VMEM], out_specs...  95.8 us
    pallas_call x1, Pallas kernels, grads_call(): pl.pallas_call(partial(grads_kernel, len(sums)), in_specs=[ANY] * 10 + [V...  88.7 us
    pallas_call x2, Pallas kernels, attn_bwd(): pl.pallas_call(bwd_kernel, grid_spec=pltpu.PrefetchScalarGridSpec(num_sca...  62 us
    pallas_call x1, Pallas kernels, pass_call(): pl.pallas_call(pass_kernel, in_specs=[ANY, VMEM, ANY, ANY, ANY, ANY, ANY]...  61.2 us
    pallas_call x1, Pallas kernels, turn_call(): pl.pallas_call(partial(turn_kernel, each), in_specs=[ANY, VMEM, VMEM, ANY...  42.9 us
    pallas_call x2, Pallas kernels, attn_fwd(): pl.pallas_call(fwd_kernel, grid_spec=pltpu.PrefetchScalarGridSpec(num_sca...  38.1 us
    pallas_call x1, Pallas kernels, first_call(): pl.pallas_call(first_kernel, in_specs=[ANY, ANY] + [VMEM] * 4, out_specs=...  30.6 us
    ppermute x2, starting transfers between devices, on_device_rows(): lax.ppermute(part, ('dp', 'seq'), pairs)  14.1 us
  transfers between devices with their start and end apart: 7, of which 1 were waited for; matrix products, arithmetic and copies ran while one was open for 0% of the time, Pallas kernels for 20%

profile of v1, /device:TPU:0, one launch (start us, length us, event | category | flops | bytes accessed | tf_op | source)
XLA Modules:
  0.0 461.2 jit_solution(545149806173603742)
XLA Ops:
  0.6 0.5 collective-permute-start
  1.2 0.0 copy-start.4
  1.2 30.6 %rows_qkv.1 = (bf16[1024,768]{1,0:T(8,128)(2,1)}, bf16[2048,384]{1,0:T(8,128)(2,1)}, bf16[2048,384]{1,0:T(8,128)(2,1)}, bf16[2048,384]{1,0:T(8,128)(2,1)}) custom-call(bf16[2,512,768]{2,1,0:T(8,128)(2,1)} %x_ref.1, bf16[768,2304]{1,0:T(8,128)(2,1)} %bitcast.38, bf16[1,768]{1,0:T(2,128)(2,1)} %refs_10_.1, bf16[1,768]{1,0:T(2,128)(2,1)} %b1.1, ...), custom_call_target="tpu_custom_call" | custom-call | tf_op jit(solution)/shard_map/rows_qkv/pallas_call | solution.py:871
  31.8 0.0 collective-permute-done
  31.9 0.1 select_reduce_fusion
  32.0 0.2 select_reduce_fusion.1
  32.2 0.5 broadcast_select_fusion
  32.7 1.3 select_convert_fusion
  34.1 19.1 %attn_fwd.2 = (bf16[2048,384]{1,0:T(8,128)(2,1)}, f32[3,8,2048]{2,1,0:T(8,128)}) custom-call(s32[8]{0:T(128)} %get-tuple-element.133.lo_ref, s32[8]{0:T(128)} %get-tuple-element.132.hi_ref, bf16[2048,384]{1,0:T(8,128)(2,1)} %get-tuple-element.73.q_ref, bf16[2048,384]{1,0:T(8,128)(2,1)} %get-tuple-element.74.k_ref, ...), custom_call_target="tpu_custom_call" | custom-call | tf_op jit(solution)/shard_map/attn_fwd/pallas_call | solution.py:417
  53.2 61.2 %ffn_pass_qkv.1 = (bf16[1024,768]{1,0:T(8,128)(2,1)}, bf16[1024,768]{1,0:T(8,128)(2,1)}, bf16[768,1024]{1,0:T(8,128)(2,1)}, bf16[2048,384]{1,0:T(8,128)(2,1)}, b...) custom-call(bf16[2048,384]{1,0:T(8,128)(2,1)} %get-tuple-element.76.o_ref, ...), custom_call_target="tpu_custom_call" | custom-call | tf_op jit(solution)/shard_map/ffn_pass_qkv/pallas_call | solution.py:1051
  114.5 19.0 %attn_fwd.3 = (bf16[2048,384]{1,0:T(8,128)(2,1)}, f32[3,8,2048]{2,1,0:T(8,128)}) custom-call(s32[8]{0:T(128)} %get-tuple-element.133.lo_ref, s32[8]{0:T(128)} %get-tuple-element.132.hi_ref, bf16[2048,384]{1,0:T(8,128)(2,1)} %get-tuple-element.78.q_ref, bf16[2048,384]{1,0:T(8,128)(2,1)} %get-tuple-element.79.k_ref, ...), custom_call_target="tpu_custom_call" | custom-call | tf_op jit(solution)/shard_map/attn_fwd/pallas_call | solution.py:417
  133.4 42.9 %ffn_turn.1 = (bf16[512,768]{1,0:T(8,128)(2,1)}, bf16[512,768]{1,0:T(8,128)(2,1)}, f32[1024,768]{1,0:T(8,128)}, bf16[1024,3072]{1,0:T(8,128)(2,1)}, bf16[768,102...) custom-call(bf16[2048,384]{1,0:T(8,128)(2,1)} %get-tuple-element.81., ...), custom_call_target="tpu_custom_call" | custom-call | tf_op jit(solution)/shard_map/ffn_turn/pallas_call | solution.py:1154
  176.3 1.8 collective-permute-start.1
  178.1 12.4 %collective-permute-start.2 = (bf16[512,768]{1,0:T(8,128)(2,1)}, bf16[512,768]{1,0:T(8,128)(2,1)S(1)}, u32[]{:S(2)}, u32[]{:S(2)}) collective-permute-start(bf16[512,768]{1,0:T(8,128)(2,1)} %get-tuple-element.88), channel_id=1, source_target_pairs={{1,0},{0,1},{5,2},{4,3},{3,4},{2,5},{7,6},{6,7},{9,8},{8,9},{13,10... | collective-permute-start | bytes 2359304 | tf_op jit(solution)/shard_map/ppermute | solution.py:1882
  190.4 31.0 %attn_bwd.2 = (bf16[2048,384]{1,0:T(8,128)(2,1)}, bf16[2048,384]{1,0:T(8,128)(2,1)}, bf16[2048,384]{1,0:T(8,128)(2,1)}) custom-call(s32[8]{0:T(128)} %get-tuple-element.133.lo_ref, s32[8]{0:T(128)} %get-tuple-element.132.hi_ref, bf16[2048,384]{1,0:T(8,128)(2,1)} %get-tuple-element.78.q_ref, bf16[2048,384]{1,0:T(8,128)(2,1)} %get-tuple-element.79.k_ref, ...), custom_call_target="tpu_custom_call" | custom-call | tf_op jit(solution)/shard_map/attn_bwd/pallas_call | solution.py:523
  221.5 0.0 collective-permute-done.1.refs_0_
  221.5 0.0 collective-permute-done.2.refs_1_
  221.5 95.8 %qkv_back_pass.1 = (bf16[2,512,768]{2,1,0:T(8,128)(2,1)}, f32[1024,768]{1,0:T(8,128)}, bf16[1024,768]{1,0:T(8,128)(2,1)}, bf16[2048,384]{1,0:T(8,128)(2,1)}, bf1...) custom-call(bf16[2048,384]{1,0:T(8,128)(2,1)} %get-tuple-element.89., ...), custom_call_target="tpu_custom_call" | custom-call | tf_op jit(solution)/shard_map/qkv_back_pass/pallas_call | solution.py:1391
  317.3 2.3 collective-permute-start.6
  319.6 0.6 collective-permute-start.3
  320.1 0.0 collective-permute-start.4
  320.1 3.3 collective-permute-start.5
  323.4 31.0 %attn_bwd.3 = (bf16[2048,384]{1,0:T(8,128)(2,1)}, bf16[2048,384]{1,0:T(8,128)(2,1)}, bf16[2048,384]{1,0:T(8,128)(2,1)}) custom-call(s32[8]{0:T(128)} %get-tuple-element.133.lo_ref, s32[8]{0:T(128)} %get-tuple-element.131.hi_ref, bf16[2048,384]{1,0:T(8,128)(2,1)} %get-tuple-element.78.q_ref, bf16[2048,384]{1,0:T(8,128)(2,1)} %get-tuple-element.79.k_ref, ...), custom_call_target="tpu_custom_call" | custom-call | tf_op jit(solution)/shard_map/attn_bwd/pallas_call | solution.py:523
  354.4 0.0 collective-permute-done.3.refs_15_
  354.4 0.0 copy-start.3
  354.4 7.7 %collective-permute-done.4.refs_16_ = bf16[96,3072]{1,0:T(8,128)(2,1)} collective-permute-done((bf16[96,3072]{1,0:T(8,128)(2,1)}, bf16[96,3072]{1,0:T(8,128)(2,1)}, u32[]{:S(2)}, u32[]{:S(2)}) %collective-permute-start.4) | collective-permute-done | bytes 589856 | tf_op jit(solution)/shard_map/ppermute | solution.py:1859
  362.2 0.0 collective-permute-done.5.refs_17_
  362.2 1.0 copy-done
  363.2 88.7 %weight_grads.1 = (f32[48,768]{1,0:T(8,128)}, f32[48,2304]{1,0:T(8,128)}, f32[48,3072]{1,0:T(8,128)}, f32[192,768]{1,0:T(8,128)}, f32[72,128]{1,0:T(8,128)}, /*index=5*/bf16[2,512,768]{2,1,0:T(8,128)(2,1)}) custom-call(bf16[2048,384]{1,0:T(8,128)(2,1)} %get-tuple-element.98.refs_0_, bf16[2048,384]{1,0:T(8,128)(2,1)} %get-tuple-element.99.refs_1_, ...), custom_call_target="tpu_custom_call" | custom-call | tf_op jit(solution)/shard_map/weight_grads/pallas_call | solution.py:1774
  451.9 1.3 dynamic_slice.39
  453.2 6.3 %finish.1 = (f32[2,512,768]{2,1,0:T(8,128)}, bf16[2,512,768]{2,1,0:T(8,128)(2,1)}, f32[48,768]{1,0:T(8,128)}, f32[48,2304]{1,0:T(8,128)}, f32[48,3072]{1,0:T(8,128)}, /*index=5*/f32[192,768]{1,0:T(8,128)}) custom-call(bf16[2,512,768]{2,1,0:T(8,128)(2,1)} %get-tuple-element.117.dx_ref, bf16[512,768]{1,0:T(8,128)(2,1)} %copy-done.1, ...), custom_call_target="tpu_custom_call" | custom-call | tf_op jit(solution)/shard_map/finish/pallas_call | solution.py:1823
  459.6 1.5 dynamic-slice_bitcast_fusion
  (17 shorter events, 0.1 us)
Async XLA Ops:
  0.6 31.2 %collective-permute-start = (s32[2,16]{1,0:T(2,128)}, s32[2,16]{1,0:T(2,128)S(1)}, u32[]{:S(2)}, u32[]{:S(2)}) collective-permute-start(s32[2,16]{1,0:T(2,128)} %param.17), channel_id=1, source_target_pairs={{0,4},{4,0},{8,12},{12,8},{1,5},{5,1},{9,13},{13,9},{2,6},{6,2},{1... | collective-permute-start | bytes 392 | tf_op jit(solution)/shard_map/ppermute | solution.py:1836
  1.2 30.6 %copy-start.4 = (s32[2,16]{1,0:T(2,128)S(1)}, s32[2,16]{1,0:T(2,128)}, u32[]{:S(2)}) copy-start(s32[2,16]{1,0:T(2,128)} %param.17) | copy-start | bytes 388
  176.3 45.2 %collective-permute-start.1 = (bf16[512,768]{1,0:T(8,128)(2,1)}, bf16[512,768]{1,0:T(8,128)(2,1)S(1)}, u32[]{:S(2)}, u32[]{:S(2)}) collective-permute-start(bf16[512,768]{1,0:T(8,128)(2,1)} %get-tuple-element.87), channel_id=1, source_target_pairs={{0,0},{1,1},{4,2},{5,3},{2,4},{3,5},{6,6},{7,7},{8,8},{9,9},{12,10... | collective-permute-start | bytes 2359304 | tf_op jit(solution)/shard_map/ppermute | solution.py:1882
  178.1 43.4 %collective-permute-start.2 = (bf16[512,768]{1,0:T(8,128)(2,1)}, bf16[512,768]{1,0:T(8,128)(2,1)S(1)}, u32[]{:S(2)}, u32[]{:S(2)}) collective-permute-start(bf16[512,768]{1,0:T(8,128)(2,1)} %get-tuple-element.88), channel_id=1, source_target_pairs={{1,0},{0,1},{5,2},{4,3},{3,4},{2,5},{7,6},{6,7},{9,8},{8,9},{13,10... | collective-permute-start | bytes 2359304 | tf_op jit(solution)/shard_map/ppermute | solution.py:1882
  221.5 95.8 %copy-start.1 = (bf16[512,768]{1,0:T(8,128)(2,1)}, bf16[512,768]{1,0:T(8,128)(2,1)S(1)}, u32[]{:S(2)}) copy-start(bf16[512,768]{1,0:T(8,128)(2,1)S(1)} %collective-permute-done.1.refs_0_) | copy-start | bytes 2359300
  221.5 95.8 %copy-start.2 = (bf16[512,768]{1,0:T(8,128)(2,1)}, bf16[512,768]{1,0:T(8,128)(2,1)S(1)}, u32[]{:S(2)}) copy-start(bf16[512,768]{1,0:T(8,128)(2,1)S(1)} %collective-permute-done.2.refs_1_) | copy-start | bytes 2359300
  317.3 44.9 %collective-permute-start.6 = (bf16[768,768]{1,0:T(8,128)(2,1)}, bf16[768,768]{1,0:T(8,128)(2,1)S(1)}, u32[]{:S(2)}, u32[]{:S(2)}) collective-permute-start(bf16[768,768]{1,0:T(8,128)(2,1)} %get-tuple-element.111), channel_id=1, source_target_pairs={{0,8},{4,12},{8,0},{12,4},{1,9},{5,13},{9,1},{13,5},{2,10},{6,14},... | collective-permute-start | bytes 3538952 | tf_op jit(solution)/shard_map/ppermute | solution.py:1854
  319.6 34.9 %collective-permute-start.3 = (bf16[96,3072]{1,0:T(8,128)(2,1)}, bf16[96,3072]{1,0:T(8,128)(2,1)S(1)}, u32[]{:S(2)}, u32[]{:S(2)}) collective-permute-start(bf16[96,3072]{1,0:T(8,128)(2,1)} %get-tuple-element.107), channel_id=1, source_target_pairs={{0,1},{1,2},{2,3},{3,0},{4,5},{5,6},{6,7},{7,4},{8,9},{9,10},{10,1... | collective-permute-start | bytes 1769480 | tf_op jit(solution)/shard_map/ppermute | solution.py:1859
  320.1 42.0 %collective-permute-start.4 = (bf16[96,3072]{1,0:T(8,128)(2,1)}, bf16[96,3072]{1,0:T(8,128)(2,1)}, u32[]{:S(2)}, u32[]{:S(2)}) collective-permute-start(bf16[96,3072]{1,0:T(8,128)(2,1)} %get-tuple-element.108), channel_id=1, source_target_pairs={{0,2},{1,3},{2,0},{3,1},{4,6},{5,7},{6,4},{7,5},{8,10},{9,11},{10,... | collective-permute-start | bytes 1769480 | tf_op jit(solution)/shard_map/ppermute | solution.py:1859
  320.1 42.0 %collective-permute-start.5 = (bf16[96,3072]{1,0:T(8,128)(2,1)}, bf16[96,3072]{1,0:T(8,128)(2,1)}, u32[]{:S(2)}, u32[]{:S(2)}) collective-permute-start(bf16[96,3072]{1,0:T(8,128)(2,1)} %get-tuple-element.109), channel_id=1, source_target_pairs={{0,3},{1,0},{2,1},{3,2},{4,7},{5,4},{6,5},{7,6},{8,11},{9,8},{10,9... | collective-permute-start | bytes 1769480 | tf_op jit(solution)/shard_map/ppermute | solution.py:1859
  354.4 7.8 %copy-start.3 = (bf16[96,3072]{1,0:T(8,128)(2,1)}, bf16[96,3072]{1,0:T(8,128)(2,1)S(1)}, u32[]{:S(2)}) copy-start(bf16[96,3072]{1,0:T(8,128)(2,1)S(1)} %collective-permute-done.3.refs_15_) | copy-start | bytes 1769476
  362.2 1.0 copy-start
